TPU v7x, 256 devices: a whole 4x4x8 slice. The times are simulated.
256 devices in a mesh: group: 64 (over z_lo, y, x, core), head: 4 (over z_hi).
Axes of the slice: x: 4, y: 4, z: 8 (z_hi: 4, z_lo: 2; z = z_hi * 2 + z_lo), core: 2. Of those that a mesh axis runs over, the one named last changes fastest.
Arguments:
- queries: bfloat16 [65536, 3072], P(('group', 'head')), may hold values from -160 to 160
- keys: bfloat16 [65536, 3072], P(('group', 'head')), may hold values from -8 to 8
- values: bfloat16 [65536, 3072], P(('group', 'head')), may hold values from -6 to 6
- noise_level: int32 [64], replicated, may hold values from 0 to 7, as said below
- tile_mask: int32 [64, 8, 16], P('group'), may hold values from 0 to 1, as said below
Outputs:
- attended: bfloat16 [65536, 3072], P(('group', 'head'))
Inputs may be any that keep to these rules, and one draw needn't show every extreme that they name: `tile_mask`: entries are 0 or 1; for every group, query tile i always sees key tiles i and 8 + i. `noise_level`: the first group is at level 0, the last at level 7, and the group before the last is at a lower level than the last.
All inputs are finite; a program needn't handle non-finite values.
Results may differ from a plain program's by a relative error of at most 0.0047.
Values may be sent and summed in bfloat16 or wider, within the bound.
No kernel may reach another device: no remote copies, remote signals or barrier semaphores. Data moves between devices by JAX's collectives and lax.ppermute only.
A program may use at most 128 MiB of HBM per device.

v0:
```python
import math

import jax
import jax.numpy as jnp
from jax import lax
from jax.sharding import PartitionSpec as P

HD = 128


def passed_along(block, axis, distance):
    devices = range(lax.axis_size(axis))
    route = [(i - distance, i) for i in devices if i - distance in devices]
    return lax.ppermute(block, axis, route)


def attend_local(query_rows, key_rows, value_rows, keep_tiles):
    rows = query_rows.shape[0]
    heads = query_rows.shape[1] // HD
    tile_size = rows // keep_tiles.shape[0]
    block = math.gcd(rows, 512)
    count = rows // block
    key_heads = key_rows.reshape(2 * rows, heads, HD)
    value_heads = value_rows.reshape(2 * rows, heads, HD)

    def one_block(index):
        query_block = lax.dynamic_slice_in_dim(query_rows, index * block, block, 0).reshape(
            block, heads, HD
        )
        mask_block = lax.dynamic_slice_in_dim(
            keep_tiles, index * (block // tile_size), block // tile_size, 0
        )
        allowed = jnp.repeat(jnp.repeat(mask_block > 0, tile_size, axis=0), tile_size, axis=1)
        scores = jnp.einsum(
            "qhd,khd->hqk", query_block, key_heads, preferred_element_type=jnp.float32
        ) / math.sqrt(HD)
        scores = jnp.where(allowed[None], scores, -jnp.inf)
        top = jnp.max(scores, axis=-1, keepdims=True)
        weights = jnp.exp(scores - top)
        total = jnp.sum(weights, axis=-1)
        probs = weights.astype(jnp.bfloat16)
        result = jnp.einsum("hqk,khd->qhd", probs, value_heads, preferred_element_type=jnp.float32)
        result = result / jnp.transpose(total)[:, :, None]
        return result.reshape(block, heads * HD).astype(jnp.bfloat16)

    blocks = lax.map(one_block, jnp.arange(count))
    return blocks.reshape(rows, heads * HD)


def shards(queries, keys, values, noise_level, tile_mask):
    query_rows, key_rows, value_rows = (
        lax.all_to_all(queries, "head", split_axis=1, concat_axis=0, tiled=True),
        lax.all_to_all(keys, "head", split_axis=1, concat_axis=0, tiled=True),
        lax.all_to_all(values, "head", split_axis=1, concat_axis=0, tiled=True),
    )
    key_old, value_old = passed_along((key_rows, value_rows), "group", 1)
    position = lax.axis_index("group")
    indices = jnp.arange(noise_level.shape[0], dtype=jnp.int32)
    own_level = jnp.sum(jnp.where(indices == position, noise_level, 0))
    prior_level = jnp.sum(jnp.where(indices == position - 1, noise_level, 0))
    see = jnp.logical_and(position > 0, prior_level < own_level).astype(jnp.int32)
    tiles = tile_mask.shape[1]
    gate = jnp.concatenate([jnp.full((tiles,), see, jnp.int32), jnp.ones((tiles,), jnp.int32)])
    keep_tiles = tile_mask[0] * gate[None, :]
    context_keys = jnp.concatenate([key_old, key_rows], axis=0)
    context_values = jnp.concatenate([value_old, value_rows], axis=0)
    result = attend_local(query_rows, context_keys, context_values, keep_tiles)
    return lax.all_to_all(result, "head", split_axis=0, concat_axis=1, tiled=True)


def solution(mesh):
    in_specs = (
        P(("group", "head"), None),
        P(("group", "head"), None),
        P(("group", "head"), None),
        P(),
        P("group", None, None),
    )
    out_specs = P(("group", "head"), None)
    return jax.shard_map(shards, mesh=mesh, in_specs=in_specs, out_specs=out_specs, check_vma=False)
```

profile of v0, /device:TPU:32, one launch (start us, length us, event | category | flops | bytes accessed | tf_op | source)
XLA Modules:
  0.0 282.9 jit_solution(13908644322788019128)
XLA Ops:
  0.0 2.7 copy.56
  2.7 7.6 %all-to-all-start.1 = ((bf16[256,4,768]{0,2,1:T(8,128)(2,1)}), bf16[256,4,768]{0,2,1:T(8,128)(2,1)S(1)}, u32[]{:S(2)}, u32[]{:S(2)}) async-start(bf16[256,4,768]{0,2,1:T(8,128)(2,1)} %bitcast.11), calls=%async_computation.1 | async-start | bytes 3145728 | tf_op jit(solution)/shard_map/all_to_all | solution.py:53
  10.3 1.6 copy.60
  11.8 37.9 %all-to-all-done.1 = bf16[256,4,768]{0,2,1:T(8,128)(2,1)S(1)} async-done(((bf16[256,4,768]{0,2,1:T(8,128)(2,1)}), bf16[256,4,768]{0,2,1:T(8,128)(2,1)S(1)}, u32[]{:S(2)}, u32[]{:S(2)}) %all-to-all-start.1) | async-done | bytes 1572896 | tf_op jit(solution)/shard_map/all_to_all | solution.py:53
  49.8 3.6 %all-to-all-start.2 = ((bf16[256,4,768]{0,2,1:T(8,128)(2,1)}), bf16[256,4,768]{0,2,1:T(8,128)(2,1)S(1)}, u32[]{:S(2)}, u32[]{:S(2)}) async-start(bf16[256,4,768]{0,2,1:T(8,128)(2,1)} %bitcast.76), calls=%async_computation.2 | async-start | bytes 3145728 | tf_op jit(solution)/shard_map/all_to_all | solution.py:54
  53.3 2.6 copy.54
  55.9 36.5 %all-to-all-done.2 = bf16[256,4,768]{0,2,1:T(8,128)(2,1)S(1)} async-done(((bf16[256,4,768]{0,2,1:T(8,128)(2,1)}), bf16[256,4,768]{0,2,1:T(8,128)(2,1)S(1)}, u32[]{:S(2)}, u32[]{:S(2)}) %all-to-all-start.2) | async-done | bytes 1572896 | tf_op jit(solution)/shard_map/all_to_all | solution.py:54
  92.4 7.3 %all-to-all-start = ((bf16[256,4,768]{0,2,1:T(8,128)(2,1)}), bf16[256,4,768]{0,2,1:T(8,128)(2,1)}, u32[]{:S(2)}, u32[]{:S(2)}) async-start(bf16[256,4,768]{0,2,1:T(8,128)(2,1)} %bitcast.75), calls=%async_computation | async-start | bytes 3145728 | tf_op jit(solution)/shard_map/all_to_all | solution.py:52
  99.8 1.6 copy.57
  101.3 1.9 collective-permute-start
  103.2 1.6 copy.61
  104.9 3.5 %collective-permute-start.1 = (bf16[1024,768]{1,0:T(8,128)(2,1)}, bf16[1024,768]{1,0:T(8,128)(2,1)}, u32[]{:S(2)}, u32[]{:S(2)}) collective-permute-start(bf16[1024,768]{1,0:T(8,128)(2,1)} %bitcast.82), channel_id=1, source_target_pairs={{0,4},{4,8},{8,12},{12,16},{16,20},{20,24},{24,28},{28,32},{32,36}... | collective-permute-start | bytes 4718600 | tf_op jit(solution)/shard_map/ppermute | solution.py:14
  108.4 0.7 fusion.12
  110.5 2.4 copy.59
  112.9 3.8 %concatenate.21 = bf16[1024,6,128]{0,2,1:T(8,128)(2,1)} reshape(bf16[4,256,768]{1,0,2:T(4,128)(2,1)} %copy.59) | data formatting | bytes 3145728 | tf_op jit(solution)/shard_map/concatenate | solution.py:65
  116.7 1.2 copy.63
  117.9 2.3 concatenate.24
  120.3 10.7 %all-to-all-done = bf16[256,4,768]{0,2,1:T(8,128)(2,1)} async-done(((bf16[256,4,768]{0,2,1:T(8,128)(2,1)}), bf16[256,4,768]{0,2,1:T(8,128)(2,1)}, u32[]{:S(2)}, u32[]{:S(2)}) %all-to-all-start) | async-done | bytes 1572896 | tf_op jit(solution)/shard_map/all_to_all | solution.py:52
  131.0 2.6 copy.55
  133.6 11.3 %collective-permute-done = bf16[1024,768]{1,0:T(8,128)(2,1)} collective-permute-done((bf16[1024,768]{1,0:T(8,128)(2,1)}, bf16[1024,768]{1,0:T(8,128)(2,1)}, u32[]{:S(2)}, u32[]{:S(2)}) %collective-permute-start) | collective-permute-done | bytes 1572896 | tf_op jit(solution)/shard_map/ppermute | solution.py:14
  144.8 2.6 copy.58
  147.4 2.1 pad_maximum_fusion
  149.6 2.8 copy.65
  152.4 9.3 %collective-permute-done.1 = bf16[1024,768]{1,0:T(8,128)(2,1)} collective-permute-done((bf16[1024,768]{1,0:T(8,128)(2,1)}, bf16[1024,768]{1,0:T(8,128)(2,1)}, u32[]{:S(2)}, u32[]{:S(2)}) %collective-permute-start.1) | collective-permute-done | bytes 1572896 | tf_op jit(solution)/shard_map/ppermute | solution.py:14
  161.7 1.7 copy.62
  163.4 2.0 pad_maximum_fusion.1
  165.5 91.0 %while.10 = (s32[]{:T(128)}, bf16[2,512,768]{2,1,0:T(8,128)(2,1)}, s32[2]{0:T(128)S(1)}, s32[8,16]{1,0:T(8,128)S(1)}, bf16[1024,768]{1,0:T(8,128)(2,1)}, /*index...) while((s32[]{:T(128)}, bf16[2,512,768]{2,1,0:T(8,128)(2,1)}, ...), condition=%wide.region_5.6_spmd, body=%wide.region_2.5_spmd.sunk | while | flops 3291211776 | bytes 121189048 | solution.py:46
  165.5 0.7 dynamic_slice.17
  166.9 3.5 %broadcast_in_dim.70 = pred[512,16,128]{2,1,0:T(8,128)(4,1)S(1)} broadcast(pred[512,16]{1,0:T(8,128)(4,1)S(1)} %bitcast.74), dimensions={0,1} | broadcast | bytes 1056768 | tf_op jit(solution)/shard_map/while/body/eval_jaxpr/broadcast_in_dim | solution.py:33
  170.4 0.6 copy.80
  171.7 1.2 constant_dynamic-slice_fusion.2
  172.9 0.3 copy.81
  173.2 12.8 %fusion.27 = (f32[6,512]{1,0:T(8,128)S(1)}, f32[6,512,2048]{2,1,0:T(8,128)}) fusion(pred[512,2048]{1,0:T(8,128)(4,1)S(1)} %bitcast.64, bf16[512,6,128]{0,2,1:T(8,128)(2,1)S(1)} %bitcast.67, bf16[2048,6,128]{2,0,1:T(8,128)(2,1)} %get-tuple-element.174), kind=kOutput, calls=%fused_computation.2.clone.1 | convolution fusion | flops 1629484032 | bytes 30158848 | tf_op jit(solution)/shard_map/while/body/eval_jaxpr/qhd,khd->hqk/dot_general | solution.py:34
  185.9 12.1 %fusion.28 = f32[6,512]{1,0:T(8,128)S(1)} fusion(f32[6,512,2048]{2,1,0:T(8,128)} %get-tuple-element.141, f32[6,512]{1,0:T(8,128)S(1)} %get-tuple-element.142, pred[512,2048]{1,0:T(8,128)(4,1)S(1)} %bitcast.65), kind=kLoop, calls=%fused_computation.3.clone.1 | loop fusion | flops 25162752 | bytes 26238976 | tf_op jit(solution)/shard_map/while/body/eval_jaxpr/reduce_sum | solution.py:40
  198.0 11.5 %fusion.29 = bf16[512,6,128]{0,2,1:T(8,128)(2,1)S(1)} fusion(bf16[2048,6,128]{0,2,1:T(8,128)(2,1)S(1)} %copy-done.1, f32[6,512,2048]{2,1,0:T(8,128)} %get-tuple-element.141, f32[6,512]{1,0:T(8,128)S(1)} %get-tuple-element.142, pred[512,2048]{1,0:T(8,128)(4,1)S(1)} %bitcast.66, f32[512,6]{0,1:T(8,128)S(1)} %bitcast.84), kind=kOutput, calls=%fused_computation.9.clone.1 | convolution fusion | flops 1636564992 | bytes 30171136 | tf_op jit(solution)/shard_map/while/body/eval_jaxpr/hqk,khd->qhd/dot_general | solution.py:42
  209.9 1.1 copy-done.4
  211.0 0.7 dynamic_slice.17
  212.4 3.5 %broadcast_in_dim.70 = pred[512,16,128]{2,1,0:T(8,128)(4,1)S(1)} broadcast(pred[512,16]{1,0:T(8,128)(4,1)S(1)} %bitcast.74), dimensions={0,1} | broadcast | bytes 1056768 | tf_op jit(solution)/shard_map/while/body/eval_jaxpr/broadcast_in_dim | solution.py:33
  215.9 0.6 copy.80
  217.2 1.2 constant_dynamic-slice_fusion.2
  218.4 0.3 copy.81
  218.7 12.8 %fusion.27 = (f32[6,512]{1,0:T(8,128)S(1)}, f32[6,512,2048]{2,1,0:T(8,128)}) fusion(pred[512,2048]{1,0:T(8,128)(4,1)S(1)} %bitcast.64, bf16[512,6,128]{0,2,1:T(8,128)(2,1)S(1)} %bitcast.67, bf16[2048,6,128]{2,0,1:T(8,128)(2,1)} %get-tuple-element.174), kind=kOutput, calls=%fused_computation.2.clone.1 | convolution fusion | flops 1629484032 | bytes 30158848 | tf_op jit(solution)/shard_map/while/body/eval_jaxpr/qhd,khd->hqk/dot_general | solution.py:34
  231.4 12.1 %fusion.28 = f32[6,512]{1,0:T(8,128)S(1)} fusion(f32[6,512,2048]{2,1,0:T(8,128)} %get-tuple-element.141, f32[6,512]{1,0:T(8,128)S(1)} %get-tuple-element.142, pred[512,2048]{1,0:T(8,128)(4,1)S(1)} %bitcast.65), kind=kLoop, calls=%fused_computation.3.clone.1 | loop fusion | flops 25162752 | bytes 26238976 | tf_op jit(solution)/shard_map/while/body/eval_jaxpr/reduce_sum | solution.py:40
  243.5 11.5 %fusion.29 = bf16[512,6,128]{0,2,1:T(8,128)(2,1)S(1)} fusion(bf16[2048,6,128]{0,2,1:T(8,128)(2,1)S(1)} %copy-done.1, f32[6,512,2048]{2,1,0:T(8,128)} %get-tuple-element.141, f32[6,512]{1,0:T(8,128)S(1)} %get-tuple-element.142, pred[512,2048]{1,0:T(8,128)(4,1)S(1)} %bitcast.66, f32[512,6]{0,1:T(8,128)S(1)} %bitcast.84), kind=kOutput, calls=%fused_computation.9.clone.1 | convolution fusion | flops 1636564992 | bytes 30171136 | tf_op jit(solution)/shard_map/while/body/eval_jaxpr/hqk,khd->qhd/dot_general | solution.py:42
  255.4 1.1 copy-done.4
  256.5 24.0 %all_to_all.76 = bf16[4,256,768]{2,1,0:T(8,128)(2,1)S(1)} all-to-all(bf16[4,256,768]{2,1,0:T(8,128)(2,1)} %bitcast.81), channel_id=1, replica_groups=mesh['group'=64,'head'=4] {'head'}, dimensions={0} | all-to-all | bytes 3145728 | tf_op jit(solution)/shard_map/all_to_all | solution.py:68
  280.5 0.7 copy.67
  281.2 1.7 copy.68
  (31 shorter events, 0.8 us)
Async XLA Ops:
  0.0 10.3 %copy-start.2 = (bf16[256,3072]{1,0:T(8,128)(2,1)S(1)}, bf16[256,3072]{1,0:T(8,128)(2,1)}, u32[]{:S(2)}) copy-start(bf16[256,3072]{1,0:T(8,128)(2,1)} %param.9) | copy-start | bytes 4718596
  2.7 47.1 %all-to-all-start.1 = ((bf16[256,4,768]{0,2,1:T(8,128)(2,1)}), bf16[256,4,768]{0,2,1:T(8,128)(2,1)S(1)}, u32[]{:S(2)}, u32[]{:S(2)}) async-start(bf16[256,4,768]{0,2,1:T(8,128)(2,1)} %bitcast.11), calls=%async_computation.1 | async-start | bytes 3145728 | tf_op jit(solution)/shard_map/all_to_all | solution.py:53
  49.8 42.6 %all-to-all-start.2 = ((bf16[256,4,768]{0,2,1:T(8,128)(2,1)}), bf16[256,4,768]{0,2,1:T(8,128)(2,1)S(1)}, u32[]{:S(2)}, u32[]{:S(2)}) async-start(bf16[256,4,768]{0,2,1:T(8,128)(2,1)} %bitcast.76), calls=%async_computation.2 | async-start | bytes 3145728 | tf_op jit(solution)/shard_map/all_to_all | solution.py:54
  92.4 38.6 %all-to-all-start = ((bf16[256,4,768]{0,2,1:T(8,128)(2,1)}), bf16[256,4,768]{0,2,1:T(8,128)(2,1)}, u32[]{:S(2)}, u32[]{:S(2)}) async-start(bf16[256,4,768]{0,2,1:T(8,128)(2,1)} %bitcast.75), calls=%async_computation | async-start | bytes 3145728 | tf_op jit(solution)/shard_map/all_to_all | solution.py:52
  99.7 8.6 %copy-start.6 = (s32[64]{0:T(128)S(1)}, s32[64]{0:T(128)}, u32[]{:S(2)}) copy-start(s32[64]{0:T(128)} %param.10) | copy-start | bytes 772
  99.7 10.7 %copy-start.5 = (s32[1,8,16]{2,1,0:T(8,128)S(1)}, s32[1,8,16]{2,1,0:T(8,128)}, u32[]{:S(2)}) copy-start(s32[1,8,16]{2,1,0:T(8,128)} %param.11) | copy-start | bytes 1540
  101.3 43.5 %collective-permute-start = (bf16[1024,768]{1,0:T(8,128)(2,1)}, bf16[1024,768]{1,0:T(8,128)(2,1)}, u32[]{:S(2)}, u32[]{:S(2)}) collective-permute-start(bf16[1024,768]{1,0:T(8,128)(2,1)} %bitcast.83), channel_id=1, source_target_pairs={{0,4},{4,8},{8,12},{12,16},{16,20},{20,24},{24,28},{28,32},{32,36}... | collective-permute-start | bytes 4718600 | tf_op jit(solution)/shard_map/ppermute | solution.py:14
  104.9 56.8 %collective-permute-start.1 = (bf16[1024,768]{1,0:T(8,128)(2,1)}, bf16[1024,768]{1,0:T(8,128)(2,1)}, u32[]{:S(2)}, u32[]{:S(2)}) collective-permute-start(bf16[1024,768]{1,0:T(8,128)(2,1)} %bitcast.82), channel_id=1, source_target_pairs={{0,4},{4,8},{8,12},{12,16},{16,20},{20,24},{24,28},{28,32},{32,36}... | collective-permute-start | bytes 4718600 | tf_op jit(solution)/shard_map/ppermute | solution.py:14
  152.4 11.0 %copy-start = (bf16[1024,6,128]{0,2,1:T(8,128)(2,1)S(1)}, bf16[1024,6,128]{0,2,1:T(8,128)(2,1)}, u32[]{:S(2)}) copy-start(bf16[1024,6,128]{0,2,1:T(8,128)(2,1)} %concatenate.24) | copy-start | bytes 4718596
  185.9 12.1 %copy-start.1 = (bf16[2048,6,128]{0,2,1:T(8,128)(2,1)S(1)}, bf16[2048,6,128]{0,2,1:T(8,128)(2,1)}, u32[]{:S(2)}) copy-start(bf16[2048,6,128]{0,2,1:T(8,128)(2,1)} %get-tuple-element.175) | copy-start | bytes 9437188 | tf_op jit(solution)/shard_map/while
  198.0 11.8 %copy-start.3 = (bf16[2,512,768]{2,1,0:T(8,128)(2,1)S(1)}, bf16[2,512,768]{2,1,0:T(8,128)(2,1)}, u32[]{:S(2)}) copy-start(bf16[2,512,768]{2,1,0:T(8,128)(2,1)} %get-tuple-element.157) | copy-start | bytes 4718596 | tf_op jit(solution)/shard_map/while
  209.8 1.1 copy-start.4
  231.4 12.1 %copy-start.1 = (bf16[2048,6,128]{0,2,1:T(8,128)(2,1)S(1)}, bf16[2048,6,128]{0,2,1:T(8,128)(2,1)}, u32[]{:S(2)}) copy-start(bf16[2048,6,128]{0,2,1:T(8,128)(2,1)} %get-tuple-element.175) | copy-start | bytes 9437188 | tf_op jit(solution)/shard_map/while
  243.5 11.8 %copy-start.3 = (bf16[2,512,768]{2,1,0:T(8,128)(2,1)S(1)}, bf16[2,512,768]{2,1,0:T(8,128)(2,1)}, u32[]{:S(2)}) copy-start(bf16[2,512,768]{2,1,0:T(8,128)(2,1)} %get-tuple-element.157) | copy-start | bytes 4718596 | tf_op jit(solution)/shard_map/while
  255.4 1.1 copy-start.4
where the time goes:
time: 284 us; the launch traced here: 283 us
  waiting for transfers between devices  106 us (37%)
  matrix products  48.4 us (17%)
  local copies, waits for them, and re-layouts  47.4 us (17%)
  other arithmetic  29.1 us (10%)
  blocking collectives  24 us (8%)
  starting transfers between devices  23.9 us (8%)
  loops' own time  3.01 us (1%)
    all_to_all x1, waiting for transfers between devices, shards(): lax.all_to_all(keys, 'head', split_axis=1, concat_axis=0, tiled=True)  37.9 us
    all_to_all x1, waiting for transfers between devices, shards(): lax.all_to_all(values, 'head', split_axis=1, concat_axis=0, tiled=True)  36.5 us
    dot_general x2, matrix products, one_block(): jnp.einsum('qhd,khd->hqk', query_block, key_heads, preferred_element_type...  25.5 us
    reduce_sum x2, other arithmetic, one_block(): total = jnp.sum(weights, axis=-1)  24.1 us
    all_to_all x1, blocking collectives, shards(): lax.all_to_all(result, 'head', split_axis=0, concat_axis=1, tiled=True)  24 us
    dot_general x2, matrix products, one_block(): jnp.einsum('hqk,khd->qhd', probs, value_heads, preferred_element_type=jnp...  22.9 us
    ppermute x2, waiting for transfers between devices, passed_along(): return lax.ppermute(block, axis, route)  20.6 us
    all_to_all x1, waiting for transfers between devices, shards(): lax.all_to_all(queries, 'head', split_axis=1, concat_axis=0, tiled=True)  10.7 us
  transfers between devices with their start and end apart: 5, of which 5 were waited for; matrix products, arithmetic and copies ran while one was open for 10% of the time, Pallas kernels for 0%

commit v1 on v0

v1 whole, which is shorter than its diff:
```python
import functools
import math

import jax
import jax.numpy as jnp
from jax import lax
from jax.experimental import pallas as pl
from jax.experimental.pallas import tpu as pltpu
from jax.sharding import PartitionSpec as P

HD = 128
TILE = 128
CHUNKS = ((2, 1), (2, 0), (2, 1))
SCALE = math.log2(math.e) / math.sqrt(HD)
ANY = pl.BlockSpec(memory_space=pl.ANY)
SMEM = pl.BlockSpec(memory_space=pltpu.SMEM)
BUSY = 1 << 36
VMEM_LIMIT = 60 * 1024 * 1024


def run_copies(pairs, stage, sems):
    count = len(pairs)
    slots = [stage.at[i] for i in range(count)]
    reads = [
        pltpu.make_async_copy(pairs[i][0], slots[i], sems.at[0, i]) for i in range(count)
    ]
    writes = [
        pltpu.make_async_copy(slots[i], pairs[i][1], sems.at[1, i]) for i in range(count)
    ]
    for read in reads:
        read.start()
    for read, write in zip(reads, writes):
        read.wait()
        write.start()
    for write in writes:
        write.wait()


def staging(count, shape):
    return [pltpu.VMEM((count, *shape), jnp.bfloat16), pltpu.SemaphoreType.DMA((2, count))]


def column(block, ways, width, start):
    return pl.multiple_of(lax.rem(block, ways) * (width // ways) + start, HD)


def turned(chunk):
    group, count = lax.axis_index("group"), lax.axis_size("group")
    return jnp.where(group >= count // 2, jnp.int32(chunk[1]), jnp.int32(0))


def spans():
    start = 0
    for chunk in CHUNKS:
        yield chunk, start * HD, chunk[0] * HD
        start += chunk[0]


def pack_body(ways, width, order, *refs):
    sources, outs, stages, sems = refs[:3], refs[3:-4], refs[-4:-1], refs[-1]
    me = lax.axis_index("head")
    block = width // ways
    copies = []
    count = len(order)
    parts = len(CHUNKS)
    for j, (chunk, start, wide) in enumerate(spans()):
        for source in (1, 2):
            for i, s in enumerate(order):
                cols = pl.ds(column(me + s + turned(chunk), ways, width, start), wide)
                slot = stages[source].at[:, pl.ds(i * block + start, wide)]
                out = outs[j * count + i].at[source - 1]
                copies.append((sources[source].at[:, cols], slot, out))
    for i, s in enumerate(order):
        for chunk, start, wide in spans():
            cols = pl.ds(column(me + s + turned(chunk), ways, width, start), wide)
            slot = stages[0].at[:, pl.ds(i * block + start, wide)]
            out = outs[parts * count + i].at[:, pl.ds(start, wide)]
            copies.append((sources[0].at[:, cols], slot, out))
    reads = [pltpu.make_async_copy(c[0], c[1], sems.at[0, i]) for i, c in enumerate(copies)]
    writes = [pltpu.make_async_copy(c[1], c[2], sems.at[1, i]) for i, c in enumerate(copies)]
    for read in reads:
        read.start()
    for read, write in zip(reads, writes):
        read.wait()
        write.start()
    for write in writes:
        write.wait()


def pack(queries, keys, values, ways, order):
    rows, width = queries.shape
    block = width // ways
    kind = queries.dtype
    shapes = []
    for _, _, wide in spans():
        shapes += [jax.ShapeDtypeStruct((2, rows, wide), kind)] * len(order)
    shapes += [jax.ShapeDtypeStruct((rows, block), kind)] * len(order)
    return pl.pallas_call(
        functools.partial(pack_body, ways, width, order),
        out_shape=shapes,
        in_specs=[ANY] * 3,
        out_specs=[ANY] * len(shapes),
        scratch_shapes=[pltpu.VMEM((rows, width), kind)] * 3
        + [pltpu.SemaphoreType.DMA((2, 3 * len(order) * len(CHUNKS)))],
        compiler_params=pltpu.CompilerParams(vmem_limit_bytes=VMEM_LIMIT),
        name="pack",
    )(queries, keys, values)


def gather_body(ways, *refs):
    pieces, out, stage, sems = refs[:ways], refs[-3], refs[-2], refs[-1]
    run_copies([(pieces[r], out.at[pl.ds(2 * r, 2)]) for r in range(ways)], stage, sems)


def gather(pieces, gates):
    ways = len(pieces)
    _, rows, wide = pieces[0].shape
    return pl.pallas_call(
        functools.partial(gather_body, ways),
        out_shape=jax.ShapeDtypeStruct((2 * ways, rows, wide), pieces[0].dtype),
        in_specs=[ANY] * (ways + len(gates)),
        out_specs=ANY,
        scratch_shapes=staging(ways, (2, rows, wide)),
        compiler_params=pltpu.CompilerParams(vmem_limit_bytes=VMEM_LIMIT),
        name="gather",
    )(*pieces, *gates)


def touch_body(*refs):
    refs[-1][0] = jnp.int32(0)


def touch(arrays):
    return pl.pallas_call(
        touch_body,
        out_shape=jax.ShapeDtypeStruct((1,), jnp.int32),
        in_specs=[ANY] * len(arrays),
        out_specs=SMEM,
        cost_estimate=pl.CostEstimate(flops=BUSY, bytes_accessed=0, transcendentals=0),
        name="touch",
    )(*arrays)


def attend_body(ways, chunk, noise, mask, *refs):
    pieces, asks, prior, outs = refs[:ways], refs[ways : 2 * ways], refs[2 * ways], refs[-ways:]
    rows = prior.shape[1]
    per = rows // TILE
    tiles = ways * per
    me, group = lax.axis_index("head"), lax.axis_index("group")
    half = lax.axis_size("group") // 2
    see = jnp.logical_and(group > 0, noise[jnp.maximum(group - 1, 0)] < noise[group])
    see = see.astype(jnp.int32)
    moved = jnp.where(group == half, turned(chunk), 0)
    first = [lax.rem(me + ways - r, ways) * per for r in range(ways)]
    before = [lax.rem(me + moved + ways - r, ways) * per for r in range(ways)]
    lane = lax.broadcasted_iota(jnp.int32, (1, rows), 1) // TILE
    context = [(prior.at[2 * p], prior.at[2 * p + 1], before[p], see) for p in range(ways)]
    context += [(pieces[p].at[0], pieces[p].at[1], tiles + first[p], 1) for p in range(ways)]

    def score(r):
        query = asks[r][...]
        scores = []
        for key, _, tile, seen in context:
            s = lax.dot_general(
                query, key[...], (((1,), (1,)), ((), ())), preferred_element_type=jnp.float32
            )
            bands = []
            for a in range(per):
                bias = jnp.full((1, rows), -jnp.inf, jnp.float32)
                for b in range(per):
                    allowed = mask[0, first[r] + a, tile + b] * seen
                    bias = jnp.where(
                        lane == b, jnp.where(allowed > 0, jnp.float32(0), -jnp.inf), bias
                    )
                bands.append(s[a * TILE : (a + 1) * TILE] + bias)
            scores.append(jnp.concatenate(bands, axis=0))
        return scores

    later = score(0)
    for r in range(ways):
        scores = later
        if r + 1 < ways:
            later = score(r + 1)
        top = functools.reduce(jnp.maximum, scores)
        top = jnp.max(top, axis=1, keepdims=True)
        total = jnp.zeros((rows, rows), jnp.float32)
        result = jnp.zeros((rows, HD), jnp.float32)
        for s, (_, value, _, _) in zip(scores, context):
            weights = jnp.exp2((s - top) * SCALE)
            total = total + weights
            result = result + jnp.dot(
                weights.astype(jnp.bfloat16), value[...], preferred_element_type=jnp.float32
            )
        total = jnp.sum(total, axis=1, keepdims=True)
        outs[r][...] = (result / total).astype(jnp.bfloat16)


def attend(noise_level, tile_mask, pieces, asks, prior, chunk, start, gates):
    ways = len(pieces)
    rows, wide = prior.shape[1:]
    heads, skip = wide // HD, start // HD
    pairs = heads * ways * rows * 2 * ways * rows
    return pl.pallas_call(
        functools.partial(attend_body, ways, chunk),
        grid=(heads,),
        out_shape=[jax.ShapeDtypeStruct((rows, wide), jnp.bfloat16)] * ways,
        in_specs=[SMEM, SMEM]
        + [pl.BlockSpec((2, rows, HD), lambda h: (0, 0, h))] * ways
        + [pl.BlockSpec((rows, HD), lambda h: (0, h + skip))] * ways
        + [pl.BlockSpec((2 * ways, rows, HD), lambda h: (0, 0, h))]
        + [ANY] * len(gates),
        out_specs=[pl.BlockSpec((rows, HD), lambda h: (0, h))] * ways,
        compiler_params=pltpu.CompilerParams(vmem_limit_bytes=VMEM_LIMIT),
        cost_estimate=pl.CostEstimate(
            flops=8 * pairs * HD, bytes_accessed=12 * ways * rows * wide, transcendentals=pairs
        ),
        name="attend",
    )(noise_level, tile_mask, *pieces, *asks, prior, *gates)


def place_body(ways, width, chunk, start, *refs):
    pieces, out, stage, sems = refs[:ways], refs[-3], refs[-2], refs[-1]
    wide = pieces[0].shape[1]
    me = lax.axis_index("head")
    run_copies(
        [
            (pieces[r], out.at[:, pl.ds(column(me + r + turned(chunk), ways, width, start), wide)])
            for r in range(ways)
        ],
        stage,
        sems,
    )


def place(pieces, width, chunk, start, earlier):
    ways = len(pieces)
    rows = pieces[0].shape[0]
    extra = [] if earlier is None else [earlier]
    return pl.pallas_call(
        functools.partial(place_body, ways, width, chunk, start),
        out_shape=jax.ShapeDtypeStruct((rows, width), pieces[0].dtype),
        in_specs=[ANY] * (ways + len(extra)),
        out_specs=ANY,
        scratch_shapes=staging(ways, pieces[0].shape),
        input_output_aliases={ways: 0} if extra else {},
        compiler_params=pltpu.CompilerParams(vmem_limit_bytes=VMEM_LIMIT),
        name="place",
    )(*pieces, *extra)


def turn(block, distance):
    if distance == 0:
        return block
    ways = lax.axis_size("head")
    return lax.ppermute(block, "head", [(i, (i + distance) % ways) for i in range(ways)])


def onward(block, chunk):
    count, ways = lax.axis_size("group"), lax.axis_size("head")
    pairs = []
    for group in range(count - 1):
        back = chunk[1] if group + 1 == count // 2 else 0
        for i in range(ways):
            pairs.append((group * ways + i, (group + 1) * ways + (i - back) % ways))
    return lax.ppermute(block, ("group", "head"), pairs)


def shards(queries, keys, values, noise_level, tile_mask):
    ways = lax.axis_size("head")
    width = queries.shape[1]
    order = (2, 1, 3, 0)
    packed = pack(queries, keys, values, ways, order)
    moved = [turn(block, order[i % ways]) for i, block in enumerate(packed)]
    parts = [
        [moved[i * ways + order.index(r)] for r in range(ways)] for i in range(1 + len(CHUNKS))
    ]
    pieces, asks = parts[:-1], parts[-1]
    gathered = []
    for part in pieces:
        gathered.append(gather(part, gathered[-1:]))
    priors = [onward(block, chunk) for block, chunk in zip(gathered, CHUNKS)]
    gates = [touch(asks)]
    out = None
    for j, (chunk, start, _) in enumerate(spans()):
        result = attend(noise_level, tile_mask, pieces[j], asks, priors[j], chunk, start, gates)
        back = [result[0]] + [turn(result[r], ways - r) for r in range(1, ways)]
        out = place(back, width, chunk, start, out)
    return out


def solution(mesh):
    split = P(("group", "head"), None)
    in_specs = (split, split, split, P(), P("group", None, None))
    return jax.shard_map(shards, mesh=mesh, in_specs=in_specs, out_specs=split, check_vma=False)
```

time: 284 us -> 209 us (0.74)
  starting transfers between devices: 23.9 us -> 73 us
  matrix products: 48.4 us -> 0 us
  local copies, waits for them, and re-layouts: 47.4 us -> 1.45 us
  Pallas kernels: 0 us -> 44.1 us
  other arithmetic: 29.1 us -> 0 us
  blocking collectives: 24 us -> 0 us
  waiting for transfers between devices: 106 us -> 89.8 us
  loops' own time: 3.01 us -> 0 us
    all_to_all x3 -> x0, waiting for transfers between devices: 85.2 us -> none  [the longest x1 37.9 us: shards(): lax.all_to_all(keys, 'head', split_axis=1, concat_axis=0, tiled=True)]
    ppermute x2 -> x24, waiting for transfers between devices: 20.6 us -> 89.8 us  [the longest x21 63 us: turn(): lax.ppermute(block, 'head', [(i, (i + distance) % ways) for i in range(wa...]
    ppermute x2 -> x24, starting transfers between devices: 5.4 us -> 73 us  [the longest x21 64.6 us: turn(): lax.ppermute(block, 'head', [(i, (i + distance) % ways) for i in range(wa...]
    dot_general x4 -> x0, matrix products: 48.4 us -> none  [the longest x2 25.5 us: one_block(): jnp.einsum('qhd,khd->hqk', query_block, key_heads, preferred_element_type...]
    pallas_call x0 -> x11, Pallas kernels: none -> 44.1 us  [the longest x3 27.1 us: attend(): pl.pallas_call(functools.partial(attend_body, ways, chunk), grid=(heads,)...]
    reduce_sum x3 -> x0, other arithmetic: 24.8 us -> none  [the longest x2 24.1 us: one_block(): total = jnp.sum(weights, axis=-1)]
    all_to_all x1 -> x0, blocking collectives: 24 us -> none  [shards(): lax.all_to_all(result, 'head', split_axis=0, concat_axis=1, tiled=True)]
    all_to_all x3 -> x0, starting transfers between devices: 18.4 us -> none  [the longest x1 7.56 us: shards(): lax.all_to_all(keys, 'head', split_axis=1, concat_axis=0, tiled=True)]
  transfers between devices with their start and end apart: 5 -> 24, of which waited for: 5 -> 8; matrix products, arithmetic and copies ran while one was open for 10% -> 0% of each run, Pallas kernels for 0% -> 18%
where the time goes in v1:
time: 209 us
  waiting for transfers between devices  89.8 us (43%)
  starting transfers between devices  73 us (35%)
  Pallas kernels  44.1 us (21%)
    ppermute x21, starting transfers between devices, turn(): lax.ppermute(block, 'head', [(i, (i + distance) % ways) for i in range(wa...  64.6 us
    ppermute x21, waiting for transfers between devices, turn(): lax.ppermute(block, 'head', [(i, (i + distance) % ways) for i in range(wa...  63 us
    pallas_call x3, Pallas kernels, attend(): pl.pallas_call(functools.partial(attend_body, ways, chunk), grid=(heads,)...  27.1 us
    ppermute x3, waiting for transfers between devices, onward(): return lax.ppermute(block, ('group', 'head'), pairs)  26.8 us
    ppermute x3, starting transfers between devices, onward(): return lax.ppermute(block, ('group', 'head'), pairs)  8.42 us
    pallas_call x3, Pallas kernels, gather(): pl.pallas_call(functools.partial(gather_body, ways), out_shape=jax.ShapeD...  6.07 us
    pallas_call x3, Pallas kernels, place(): pl.pallas_call(functools.partial(place_body, ways, width, chunk, start),...  5.45 us
    pallas_call x1, Pallas kernels, pack(): pl.pallas_call(functools.partial(pack_body, ways, width, order), out_shap...  4.96 us
  transfers between devices with their start and end apart: 24, of which 8 were waited for; matrix products, arithmetic and copies ran while one was open for 0% of the time, Pallas kernels for 18%

profile of v1, /device:TPU:32, one launch (start us, length us, event | category | flops | bytes accessed | tf_op | source)
XLA Modules:
  0.0 208.9 jit_solution(5666846813664767161)
XLA Ops:
  0.0 5.0 %pack.1 = (bf16[2,256,256]{2,1,0:T(8,128)(2,1)}, bf16[2,256,256]{2,1,0:T(8,128)(2,1)}, bf16[2,256,256]{2,1,0:T(8,128)(2,1)}, bf16[2,256,256]{2,1,0:T(8,128)(2,1)...) custom-call(bf16[256,3072]{1,0:T(8,128)(2,1)} %refs_0_.1, ...), custom_call_target="tpu_custom_call" | custom-call | tf_op jit(solution)/shard_map/pack/pallas_call | solution.py:98
  5.0 6.4 %collective-permute-start.10 = (bf16[2,256,256]{2,1,0:T(8,128)(2,1)}, bf16[2,256,256]{2,1,0:T(8,128)(2,1)S(1)}, u32[]{:S(2)}, u32[]{:S(2)}) collective-permute-start(bf16[2,256,256]{2,1,0:T(8,128)(2,1)} %get-tuple-element.47), channel_id=1, source_target_pairs={{0,2},{1,3},{2,0},{3,1},{4,6},{5,7},{6,4},{7,5},{8,10},{9,11},{10,... | collective-permute-start | bytes 786440 | tf_op jit(solution)/shard_map/ppermute | solution.py:255
  11.3 0.6 collective-permute-start.11
  11.9 2.4 %collective-permute-start.9 = (bf16[2,256,256]{2,1,0:T(8,128)(2,1)}, bf16[2,256,256]{2,1,0:T(8,128)(2,1)S(1)}, u32[]{:S(2)}, u32[]{:S(2)}) collective-permute-start(bf16[2,256,256]{2,1,0:T(8,128)(2,1)} %get-tuple-element.46), channel_id=1, source_target_pairs={{0,1},{1,2},{2,3},{3,0},{4,5},{5,6},{6,7},{7,4},{8,9},{9,10},{10,1... | collective-permute-start | bytes 786440 | tf_op jit(solution)/shard_map/ppermute | solution.py:255
  14.3 2.7 %collective-permute-start.6 = (bf16[2,256,256]{2,1,0:T(8,128)(2,1)}, bf16[2,256,256]{2,1,0:T(8,128)(2,1)S(1)}, u32[]{:S(2)}, u32[]{:S(2)}) collective-permute-start(bf16[2,256,256]{2,1,0:T(8,128)(2,1)} %get-tuple-element.42), channel_id=1, source_target_pairs={{0,1},{1,2},{2,3},{3,0},{4,5},{5,6},{6,7},{7,4},{8,9},{9,10},{10,1... | collective-permute-start | bytes 786440 | tf_op jit(solution)/shard_map/ppermute | solution.py:255
  17.0 1.4 collective-permute-start.7
  18.4 7.4 %collective-permute-done.10.refs_2_ = bf16[2,256,256]{2,1,0:T(8,128)(2,1)S(1)} collective-permute-done((bf16[2,256,256]{2,1,0:T(8,128)(2,1)}, bf16[2,256,256]{2,1,0:T(8,128)(2,1)S(1)}, u32[]{:S(2)}, u32[]{:S(2)}) %collective-permute-start.10) | collective-permute-done | bytes 262176 | tf_op jit(solution)/shard_map/ppermute | solution.py:255
  25.8 2.5 %collective-permute-start.8 = (bf16[2,256,256]{2,1,0:T(8,128)(2,1)}, bf16[2,256,256]{2,1,0:T(8,128)(2,1)S(1)}, u32[]{:S(2)}, u32[]{:S(2)}) collective-permute-start(bf16[2,256,256]{2,1,0:T(8,128)(2,1)} %get-tuple-element.44), channel_id=1, source_target_pairs={{0,3},{1,0},{2,1},{3,2},{4,7},{5,4},{6,5},{7,6},{8,11},{9,8},{10,9... | collective-permute-start | bytes 786440 | tf_op jit(solution)/shard_map/ppermute | solution.py:255
  28.3 3.6 %collective-permute-done.11.refs_3_ = bf16[2,256,256]{2,1,0:T(8,128)(2,1)S(1)} collective-permute-done((bf16[2,256,256]{2,1,0:T(8,128)(2,1)}, bf16[2,256,256]{2,1,0:T(8,128)(2,1)S(1)}, u32[]{:S(2)}, u32[]{:S(2)}) %collective-permute-start.11) | collective-permute-done | bytes 262176 | tf_op jit(solution)/shard_map/ppermute | solution.py:255
  31.9 0.5 collective-permute-start
  32.5 16.1 %collective-permute-done.9.refs_1_ = bf16[2,256,256]{2,1,0:T(8,128)(2,1)S(1)} collective-permute-done((bf16[2,256,256]{2,1,0:T(8,128)(2,1)}, bf16[2,256,256]{2,1,0:T(8,128)(2,1)S(1)}, u32[]{:S(2)}, u32[]{:S(2)}) %collective-permute-start.9) | collective-permute-done | bytes 262176 | tf_op jit(solution)/shard_map/ppermute | solution.py:255
  48.6 2.4 %collective-permute-start.3 = (bf16[256,768]{1,0:T(8,128)(2,1)}, bf16[256,768]{1,0:T(8,128)(2,1)}, u32[]{:S(2)}, u32[]{:S(2)}) collective-permute-start(bf16[256,768]{1,0:T(8,128)(2,1)} %get-tuple-element.38), channel_id=1, source_target_pairs={{0,1},{1,2},{2,3},{3,0},{4,5},{5,6},{6,7},{7,4},{8,9},{9,10},{10,1... | collective-permute-start | bytes 1179656 | tf_op jit(solution)/shard_map/ppermute | solution.py:255
  51.0 4.9 %collective-permute-done.6.refs_1_ = bf16[2,256,256]{2,1,0:T(8,128)(2,1)S(1)} collective-permute-done((bf16[2,256,256]{2,1,0:T(8,128)(2,1)}, bf16[2,256,256]{2,1,0:T(8,128)(2,1)S(1)}, u32[]{:S(2)}, u32[]{:S(2)}) %collective-permute-start.6) | collective-permute-done | bytes 262176 | tf_op jit(solution)/shard_map/ppermute | solution.py:255
  56.0 5.5 %collective-permute-start.4 = (bf16[256,768]{1,0:T(8,128)(2,1)}, bf16[256,768]{1,0:T(8,128)(2,1)}, u32[]{:S(2)}, u32[]{:S(2)}) collective-permute-start(bf16[256,768]{1,0:T(8,128)(2,1)} %get-tuple-element.39), channel_id=1, source_target_pairs={{0,2},{1,3},{2,0},{3,1},{4,6},{5,7},{6,4},{7,5},{8,10},{9,11},{10,... | collective-permute-start | bytes 1179656 | tf_op jit(solution)/shard_map/ppermute | solution.py:255
  61.5 0.0 collective-permute-done.7.refs_2_
  61.5 0.5 collective-permute-start.5
  62.0 0.5 collective-permute-start.1
  62.5 0.2 collective-permute-done.refs_1_
  62.6 5.3 %collective-permute-start.2 = (bf16[2,256,256]{2,1,0:T(8,128)(2,1)}, bf16[2,256,256]{2,1,0:T(8,128)(2,1)S(1)}, u32[]{:S(2)}, u32[]{:S(2)}) collective-permute-start(bf16[2,256,256]{2,1,0:T(8,128)(2,1)} %get-tuple-element.36), channel_id=1, source_target_pairs={{0,3},{1,0},{2,1},{3,2},{4,7},{5,4},{6,5},{7,6},{8,11},{9,8},{10,9... | collective-permute-start | bytes 786440 | tf_op jit(solution)/shard_map/ppermute | solution.py:255
  68.0 2.0 gather.3.refs_4_
  70.0 0.0 copy-start
  70.0 2.1 %gather.4.refs_4_ = bf16[8,256,256]{2,1,0:T(8,128)(2,1)} custom-call(bf16[2,256,256]{2,1,0:T(8,128)(2,1)} %get-tuple-element.41.refs_0_, bf16[2,256,256]{2,1,0:T(8,128)(2,1)} %copy-done.2, bf16[2,256,256]{2,1,0:T(8,128)(2,1)} %copy-done.3, bf16[2,256,256]{2,1,0:T(8,128)(2,1)} %copy-done.4, bf16[8,256,256]{2,1,0:T(8,128)(2,1)} %gather.3.refs_4_), custom_call_target="tpu_custom_call" | custom-call | tf_op jit(solution)/shard_map/gather/pallas_call | solution.py:118
  72.2 28.5 %collective-permute-done.1.refs_2_ = bf16[2,256,256]{2,1,0:T(8,128)(2,1)S(1)} collective-permute-done((bf16[2,256,256]{2,1,0:T(8,128)(2,1)}, bf16[2,256,256]{2,1,0:T(8,128)(2,1)S(1)}, u32[]{:S(2)}, u32[]{:S(2)}) %collective-permute-start.1) | collective-permute-done | bytes 262176 | tf_op jit(solution)/shard_map/ppermute | solution.py:255
  100.7 1.9 collective-permute-start.20
  102.6 4.4 %collective-permute-start.16 = (bf16[8,256,256]{2,1,0:T(8,128)(2,1)}, bf16[8,256,256]{2,1,0:T(8,128)(2,1)}, u32[]{:S(2)}, u32[]{:S(2)}) collective-permute-start(bf16[8,256,256]{2,1,0:T(8,128)(2,1)} %gather.4.refs_4_), channel_id=1, source_target_pairs={{0,4},{1,5},{2,6},{3,7},{4,8},{5,9},{6,10},{7,11},{8,12},{9,13},{1... | collective-permute-start | bytes 3145736 | tf_op jit(solution)/shard_map/ppermute | solution.py:265
  107.1 2.0 gather.5
  109.1 2.1 %collective-permute-start.12 = (bf16[8,256,256]{2,1,0:T(8,128)(2,1)}, bf16[8,256,256]{2,1,0:T(8,128)(2,1)S(1)}, u32[]{:S(2)}, u32[]{:S(2)}) collective-permute-start(bf16[8,256,256]{2,1,0:T(8,128)(2,1)} %gather.5), channel_id=1, source_target_pairs={{0,4},{1,5},{2,6},{3,7},{4,8},{5,9},{6,10},{7,11},{8,12},{9,13},{1... | collective-permute-start | bytes 3145736 | tf_op jit(solution)/shard_map/ppermute | solution.py:265
  111.2 0.5 touch.1.refs_9_
  111.7 26.8 %collective-permute-done.20.refs_8_ = bf16[8,256,256]{2,1,0:T(8,128)(2,1)} collective-permute-done((bf16[8,256,256]{2,1,0:T(8,128)(2,1)S(1)}, bf16[8,256,256]{2,1,0:T(8,128)(2,1)}, u32[]{:S(2)}, u32[]{:S(2)}) %collective-permute-start.20) | collective-permute-done | bytes 1048608 | tf_op jit(solution)/shard_map/ppermute | solution.py:265
  138.5 9.0 %attend.5 = (bf16[256,256]{1,0:T(8,128)(2,1)}, bf16[256,256]{1,0:T(8,128)(2,1)}, bf16[256,256]{1,0:T(8,128)(2,1)}, bf16[256,256]{1,0:T(8,128)(2,1)}) custom-call(s32[64]{0:T(128)} %noise.5, s32[1,8,16]{2,1,0:T(8,128)} %mask.5, bf16[2,256,256]{2,1,0:T(8,128)(2,1)} %get-tuple-element.45.refs_0_, bf16[2,256,256]{2,1,0:T(8,128)(2,1)} %copy-done.9, ...), custom_call_target="tpu_custom_call" | custom-call | flops 4294967296 | bytes 3145728 | tf_op jit(solution)/shard_map/attend/pallas_call | solution.py:203
  147.5 17.1 %collective-permute-start.21 = (bf16[256,256]{1,0:T(8,128)(2,1)}, bf16[256,256]{1,0:T(8,128)(2,1)S(1)}, u32[]{:S(2)}, u32[]{:S(2)}) collective-permute-start(bf16[256,256]{1,0:T(8,128)(2,1)} %get-tuple-element.58), channel_id=1, source_target_pairs={{0,3},{1,0},{2,1},{3,2},{4,7},{5,4},{6,5},{7,6},{8,11},{9,8},{10,9... | collective-permute-start | bytes 393224 | tf_op jit(solution)/shard_map/ppermute | solution.py:255
  164.6 2.5 %collective-permute-start.23 = (bf16[256,256]{1,0:T(8,128)(2,1)}, bf16[256,256]{1,0:T(8,128)(2,1)S(1)}, u32[]{:S(2)}, u32[]{:S(2)}) collective-permute-start(bf16[256,256]{1,0:T(8,128)(2,1)} %get-tuple-element.60), channel_id=1, source_target_pairs={{0,1},{1,2},{2,3},{3,0},{4,5},{5,6},{6,7},{7,4},{8,9},{9,10},{10,1... | collective-permute-start | bytes 393224 | tf_op jit(solution)/shard_map/ppermute | solution.py:255
  167.1 9.0 %attend.4 = (bf16[256,256]{1,0:T(8,128)(2,1)}, bf16[256,256]{1,0:T(8,128)(2,1)}, bf16[256,256]{1,0:T(8,128)(2,1)}, bf16[256,256]{1,0:T(8,128)(2,1)}) custom-call(s32[64]{0:T(128)} %noise.5, s32[1,8,16]{2,1,0:T(8,128)} %mask.5, bf16[2,256,256]{2,1,0:T(8,128)(2,1)} %get-tuple-element.41.refs_0_, bf16[2,256,256]{2,1,0:T(8,128)(2,1)} %copy-done.2, ...), custom_call_target="tpu_custom_call" | custom-call | flops 4294967296 | bytes 3145728 | tf_op jit(solution)/shard_map/attend/pallas_call | solution.py:203
  176.1 1.8 collective-permute-start.17
  177.9 5.9 %collective-permute-start.18 = (bf16[256,256]{1,0:T(8,128)(2,1)}, bf16[256,256]{1,0:T(8,128)(2,1)S(1)}, u32[]{:S(2)}, u32[]{:S(2)}) collective-permute-start(bf16[256,256]{1,0:T(8,128)(2,1)} %get-tuple-element.55), channel_id=1, source_target_pairs={{0,2},{1,3},{2,0},{3,1},{4,6},{5,7},{6,4},{7,5},{8,10},{9,11},{10,... | collective-permute-start | bytes 393224 | tf_op jit(solution)/shard_map/ppermute | solution.py:255
  183.8 9.0 %attend.3 = (bf16[256,256]{1,0:T(8,128)(2,1)}, bf16[256,256]{1,0:T(8,128)(2,1)}, bf16[256,256]{1,0:T(8,128)(2,1)}, bf16[256,256]{1,0:T(8,128)(2,1)}) custom-call(s32[64]{0:T(128)} %noise.5, s32[1,8,16]{2,1,0:T(8,128)} %mask.5, bf16[2,256,256]{2,1,0:T(8,128)(2,1)} %get-tuple-element.33.refs_0_, bf16[2,256,256]{2,1,0:T(8,128)(2,1)} %copy-done.1, ...), custom_call_target="tpu_custom_call" | custom-call | flops 4294967296 | bytes 3145728 | tf_op jit(solution)/shard_map/attend/pallas_call | solution.py:203
  192.9 0.1 collective-permute-start.19
  193.0 4.1 %collective-permute-start.13 = (bf16[256,256]{1,0:T(8,128)(2,1)}, bf16[256,256]{1,0:T(8,128)(2,1)S(1)}, u32[]{:S(2)}, u32[]{:S(2)}) collective-permute-start(bf16[256,256]{1,0:T(8,128)(2,1)} %get-tuple-element.50), channel_id=1, source_target_pairs={{0,3},{1,0},{2,1},{3,2},{4,7},{5,4},{6,5},{7,6},{8,11},{9,8},{10,9... | collective-permute-start | bytes 393224 | tf_op jit(solution)/shard_map/ppermute | solution.py:255
  197.1 1.0 collective-permute-start.14
  198.1 1.5 collective-permute-start.15
  199.6 1.8 place.3.refs_4_
  201.5 0.6 copy-done.14
  202.1 0.1 copy-done.17
  202.1 1.8 place.4.refs_4_
  204.0 2.2 %collective-permute-done.14.refs_2_ = bf16[256,256]{1,0:T(8,128)(2,1)S(1)} collective-permute-done((bf16[256,256]{1,0:T(8,128)(2,1)}, bf16[256,256]{1,0:T(8,128)(2,1)S(1)}, u32[]{:S(2)}, u32[]{:S(2)}) %collective-permute-start.14) | collective-permute-done | bytes 131104 | tf_op jit(solution)/shard_map/ppermute | solution.py:255
  206.2 0.6 copy-done.16
  206.8 0.1 copy-done.18
  206.9 1.8 place.5
  (53 shorter events, 0.1 us)
Async XLA Ops:
  5.0 20.8 %collective-permute-start.10 = (bf16[2,256,256]{2,1,0:T(8,128)(2,1)}, bf16[2,256,256]{2,1,0:T(8,128)(2,1)S(1)}, u32[]{:S(2)}, u32[]{:S(2)}) collective-permute-start(bf16[2,256,256]{2,1,0:T(8,128)(2,1)} %get-tuple-element.47), channel_id=1, source_target_pairs={{0,2},{1,3},{2,0},{3,1},{4,6},{5,7},{6,4},{7,5},{8,10},{9,11},{10,... | collective-permute-start | bytes 786440 | tf_op jit(solution)/shard_map/ppermute | solution.py:255
  11.3 20.6 %collective-permute-start.11 = (bf16[2,256,256]{2,1,0:T(8,128)(2,1)}, bf16[2,256,256]{2,1,0:T(8,128)(2,1)S(1)}, u32[]{:S(2)}, u32[]{:S(2)}) collective-permute-start(bf16[2,256,256]{2,1,0:T(8,128)(2,1)} %get-tuple-element.48), channel_id=1, source_target_pairs={{0,3},{1,0},{2,1},{3,2},{4,7},{5,4},{6,5},{7,6},{8,11},{9,8},{10,9... | collective-permute-start | bytes 786440 | tf_op jit(solution)/shard_map/ppermute | solution.py:255
  11.9 36.7 %collective-permute-start.9 = (bf16[2,256,256]{2,1,0:T(8,128)(2,1)}, bf16[2,256,256]{2,1,0:T(8,128)(2,1)S(1)}, u32[]{:S(2)}, u32[]{:S(2)}) collective-permute-start(bf16[2,256,256]{2,1,0:T(8,128)(2,1)} %get-tuple-element.46), channel_id=1, source_target_pairs={{0,1},{1,2},{2,3},{3,0},{4,5},{5,6},{6,7},{7,4},{8,9},{9,10},{10,1... | collective-permute-start | bytes 786440 | tf_op jit(solution)/shard_map/ppermute | solution.py:255
  14.3 41.7 %collective-permute-start.6 = (bf16[2,256,256]{2,1,0:T(8,128)(2,1)}, bf16[2,256,256]{2,1,0:T(8,128)(2,1)S(1)}, u32[]{:S(2)}, u32[]{:S(2)}) collective-permute-start(bf16[2,256,256]{2,1,0:T(8,128)(2,1)} %get-tuple-element.42), channel_id=1, source_target_pairs={{0,1},{1,2},{2,3},{3,0},{4,5},{5,6},{6,7},{7,4},{8,9},{9,10},{10,1... | collective-permute-start | bytes 786440 | tf_op jit(solution)/shard_map/ppermute | solution.py:255
  17.0 44.5 %collective-permute-start.7 = (bf16[2,256,256]{2,1,0:T(8,128)(2,1)}, bf16[2,256,256]{2,1,0:T(8,128)(2,1)S(1)}, u32[]{:S(2)}, u32[]{:S(2)}) collective-permute-start(bf16[2,256,256]{2,1,0:T(8,128)(2,1)} %get-tuple-element.43), channel_id=1, source_target_pairs={{0,2},{1,3},{2,0},{3,1},{4,6},{5,7},{6,4},{7,5},{8,10},{9,11},{10,... | collective-permute-start | bytes 786440 | tf_op jit(solution)/shard_map/ppermute | solution.py:255
  25.8 42.2 %copy-start.7 = (bf16[2,256,256]{2,1,0:T(8,128)(2,1)}, bf16[2,256,256]{2,1,0:T(8,128)(2,1)S(1)}, u32[]{:S(2)}) copy-start(bf16[2,256,256]{2,1,0:T(8,128)(2,1)S(1)} %collective-permute-done.10.refs_2_) | copy-start | bytes 786436
  25.8 36.2 %collective-permute-start.8 = (bf16[2,256,256]{2,1,0:T(8,128)(2,1)}, bf16[2,256,256]{2,1,0:T(8,128)(2,1)S(1)}, u32[]{:S(2)}, u32[]{:S(2)}) collective-permute-start(bf16[2,256,256]{2,1,0:T(8,128)(2,1)} %get-tuple-element.44), channel_id=1, source_target_pairs={{0,3},{1,0},{2,1},{3,2},{4,7},{5,4},{6,5},{7,6},{8,11},{9,8},{10,9... | collective-permute-start | bytes 786440 | tf_op jit(solution)/shard_map/ppermute | solution.py:255
  31.9 36.1 %copy-start.8 = (bf16[2,256,256]{2,1,0:T(8,128)(2,1)}, bf16[2,256,256]{2,1,0:T(8,128)(2,1)S(1)}, u32[]{:S(2)}) copy-start(bf16[2,256,256]{2,1,0:T(8,128)(2,1)S(1)} %collective-permute-done.11.refs_3_) | copy-start | bytes 786436
  31.9 30.7 %collective-permute-start = (bf16[2,256,256]{2,1,0:T(8,128)(2,1)}, bf16[2,256,256]{2,1,0:T(8,128)(2,1)S(1)}, u32[]{:S(2)}, u32[]{:S(2)}) collective-permute-start(bf16[2,256,256]{2,1,0:T(8,128)(2,1)} %get-tuple-element.34), channel_id=1, source_target_pairs={{0,1},{1,2},{2,3},{3,0},{4,5},{5,6},{6,7},{7,4},{8,9},{9,10},{10,1... | collective-permute-start | bytes 786440 | tf_op jit(solution)/shard_map/ppermute | solution.py:255
  48.6 19.4 %copy-start.9 = (bf16[2,256,256]{2,1,0:T(8,128)(2,1)}, bf16[2,256,256]{2,1,0:T(8,128)(2,1)S(1)}, u32[]{:S(2)}) copy-start(bf16[2,256,256]{2,1,0:T(8,128)(2,1)S(1)} %collective-permute-done.9.refs_1_) | copy-start | bytes 786436
  48.6 60.5 %collective-permute-start.3 = (bf16[256,768]{1,0:T(8,128)(2,1)}, bf16[256,768]{1,0:T(8,128)(2,1)}, u32[]{:S(2)}, u32[]{:S(2)}) collective-permute-start(bf16[256,768]{1,0:T(8,128)(2,1)} %get-tuple-element.38), channel_id=1, source_target_pairs={{0,1},{1,2},{2,3},{3,0},{4,5},{5,6},{6,7},{7,4},{8,9},{9,10},{10,1... | collective-permute-start | bytes 1179656 | tf_op jit(solution)/shard_map/ppermute | solution.py:255
  56.0 14.0 %copy-start.2 = (bf16[2,256,256]{2,1,0:T(8,128)(2,1)}, bf16[2,256,256]{2,1,0:T(8,128)(2,1)S(1)}, u32[]{:S(2)}) copy-start(bf16[2,256,256]{2,1,0:T(8,128)(2,1)S(1)} %collective-permute-done.6.refs_1_) | copy-start | bytes 786436
  56.0 55.2 %collective-permute-start.4 = (bf16[256,768]{1,0:T(8,128)(2,1)}, bf16[256,768]{1,0:T(8,128)(2,1)}, u32[]{:S(2)}, u32[]{:S(2)}) collective-permute-start(bf16[256,768]{1,0:T(8,128)(2,1)} %get-tuple-element.39), channel_id=1, source_target_pairs={{0,2},{1,3},{2,0},{3,1},{4,6},{5,7},{6,4},{7,5},{8,10},{9,11},{10,... | collective-permute-start | bytes 1179656 | tf_op jit(solution)/shard_map/ppermute | solution.py:255
  61.5 8.5 %copy-start.3 = (bf16[2,256,256]{2,1,0:T(8,128)(2,1)}, bf16[2,256,256]{2,1,0:T(8,128)(2,1)S(1)}, u32[]{:S(2)}) copy-start(bf16[2,256,256]{2,1,0:T(8,128)(2,1)S(1)} %collective-permute-done.7.refs_2_) | copy-start | bytes 786436
  61.5 49.7 %collective-permute-start.5 = (bf16[256,768]{1,0:T(8,128)(2,1)}, bf16[256,768]{1,0:T(8,128)(2,1)}, u32[]{:S(2)}, u32[]{:S(2)}) collective-permute-start(bf16[256,768]{1,0:T(8,128)(2,1)} %get-tuple-element.40), channel_id=1, source_target_pairs={{0,3},{1,0},{2,1},{3,2},{4,7},{5,4},{6,5},{7,6},{8,11},{9,8},{10,9... | collective-permute-start | bytes 1179656 | tf_op jit(solution)/shard_map/ppermute | solution.py:255
  62.0 8.0 %copy-start.4 = (bf16[2,256,256]{2,1,0:T(8,128)(2,1)}, bf16[2,256,256]{2,1,0:T(8,128)(2,1)S(1)}, u32[]{:S(2)}) copy-start(bf16[2,256,256]{2,1,0:T(8,128)(2,1)S(1)} %collective-permute-done.8.refs_3_) | copy-start | bytes 786436
  62.0 38.7 %collective-permute-start.1 = (bf16[2,256,256]{2,1,0:T(8,128)(2,1)}, bf16[2,256,256]{2,1,0:T(8,128)(2,1)S(1)}, u32[]{:S(2)}, u32[]{:S(2)}) collective-permute-start(bf16[2,256,256]{2,1,0:T(8,128)(2,1)} %get-tuple-element.35), channel_id=1, source_target_pairs={{0,2},{1,3},{2,0},{3,1},{4,6},{5,7},{6,4},{7,5},{8,10},{9,11},{10,... | collective-permute-start | bytes 786440 | tf_op jit(solution)/shard_map/ppermute | solution.py:255
  62.6 9.5 %copy-start.1 = (bf16[2,256,256]{2,1,0:T(8,128)(2,1)}, bf16[2,256,256]{2,1,0:T(8,128)(2,1)S(1)}, u32[]{:S(2)}) copy-start(bf16[2,256,256]{2,1,0:T(8,128)(2,1)S(1)} %collective-permute-done.refs_1_) | copy-start | bytes 786436
  62.6 40.0 %collective-permute-start.2 = (bf16[2,256,256]{2,1,0:T(8,128)(2,1)}, bf16[2,256,256]{2,1,0:T(8,128)(2,1)S(1)}, u32[]{:S(2)}, u32[]{:S(2)}) collective-permute-start(bf16[2,256,256]{2,1,0:T(8,128)(2,1)} %get-tuple-element.36), channel_id=1, source_target_pairs={{0,3},{1,0},{2,1},{3,2},{4,7},{5,4},{6,5},{7,6},{8,11},{9,8},{10,9... | collective-permute-start | bytes 786440 | tf_op jit(solution)/shard_map/ppermute | solution.py:255
  70.0 30.7 %copy-start = (bf16[8,256,256]{2,1,0:T(8,128)(2,1)S(1)}, bf16[8,256,256]{2,1,0:T(8,128)(2,1)}, u32[]{:S(2)}) copy-start(bf16[8,256,256]{2,1,0:T(8,128)(2,1)} %gather.3.refs_4_) | copy-start | bytes 3145732
  100.7 6.4 %copy-start.5 = (bf16[2,256,256]{2,1,0:T(8,128)(2,1)}, bf16[2,256,256]{2,1,0:T(8,128)(2,1)S(1)}, u32[]{:S(2)}) copy-start(bf16[2,256,256]{2,1,0:T(8,128)(2,1)S(1)} %collective-permute-done.1.refs_2_) | copy-start | bytes 786436
  100.7 37.8 %collective-permute-start.20 = (bf16[8,256,256]{2,1,0:T(8,128)(2,1)S(1)}, bf16[8,256,256]{2,1,0:T(8,128)(2,1)}, u32[]{:S(2)}, u32[]{:S(2)}) collective-permute-start(bf16[8,256,256]{2,1,0:T(8,128)(2,1)S(1)} %copy-done), channel_id=1, source_target_pairs={{0,4},{1,5},{2,6},{3,7},{4,8},{5,9},{6,10},{7,11},{8,12},{9,13},{1... | collective-permute-start | bytes 3145736 | tf_op jit(solution)/shard_map/ppermute | solution.py:265
  102.6 4.4 %copy-start.6 = (bf16[2,256,256]{2,1,0:T(8,128)(2,1)}, bf16[2,256,256]{2,1,0:T(8,128)(2,1)S(1)}, u32[]{:S(2)}) copy-start(bf16[2,256,256]{2,1,0:T(8,128)(2,1)S(1)} %collective-permute-done.2.refs_3_) | copy-start | bytes 786436
  102.6 64.4 %collective-permute-start.16 = (bf16[8,256,256]{2,1,0:T(8,128)(2,1)}, bf16[8,256,256]{2,1,0:T(8,128)(2,1)}, u32[]{:S(2)}, u32[]{:S(2)}) collective-permute-start(bf16[8,256,256]{2,1,0:T(8,128)(2,1)} %gather.4.refs_4_), channel_id=1, source_target_pairs={{0,4},{1,5},{2,6},{3,7},{4,8},{5,9},{6,10},{7,11},{8,12},{9,13},{1... | collective-permute-start | bytes 3145736 | tf_op jit(solution)/shard_map/ppermute | solution.py:265
  109.1 68.8 %collective-permute-start.12 = (bf16[8,256,256]{2,1,0:T(8,128)(2,1)}, bf16[8,256,256]{2,1,0:T(8,128)(2,1)S(1)}, u32[]{:S(2)}, u32[]{:S(2)}) collective-permute-start(bf16[8,256,256]{2,1,0:T(8,128)(2,1)} %gather.5), channel_id=1, source_target_pairs={{0,4},{1,5},{2,6},{3,7},{4,8},{5,9},{6,10},{7,11},{8,12},{9,13},{1... | collective-permute-start | bytes 3145736 | tf_op jit(solution)/shard_map/ppermute | solution.py:265
  147.5 45.3 %collective-permute-start.21 = (bf16[256,256]{1,0:T(8,128)(2,1)}, bf16[256,256]{1,0:T(8,128)(2,1)S(1)}, u32[]{:S(2)}, u32[]{:S(2)}) collective-permute-start(bf16[256,256]{1,0:T(8,128)(2,1)} %get-tuple-element.58), channel_id=1, source_target_pairs={{0,3},{1,0},{2,1},{3,2},{4,7},{5,4},{6,5},{7,6},{8,11},{9,8},{10,9... | collective-permute-start | bytes 393224 | tf_op jit(solution)/shard_map/ppermute | solution.py:255
  164.6 28.4 %collective-permute-start.22 = (bf16[256,256]{1,0:T(8,128)(2,1)}, bf16[256,256]{1,0:T(8,128)(2,1)S(1)}, u32[]{:S(2)}, u32[]{:S(2)}) collective-permute-start(bf16[256,256]{1,0:T(8,128)(2,1)} %get-tuple-element.59), channel_id=1, source_target_pairs={{0,2},{1,3},{2,0},{3,1},{4,6},{5,7},{6,4},{7,5},{8,10},{9,11},{10,... | collective-permute-start | bytes 393224 | tf_op jit(solution)/shard_map/ppermute | solution.py:255
  164.6 32.5 %collective-permute-start.23 = (bf16[256,256]{1,0:T(8,128)(2,1)}, bf16[256,256]{1,0:T(8,128)(2,1)S(1)}, u32[]{:S(2)}, u32[]{:S(2)}) collective-permute-start(bf16[256,256]{1,0:T(8,128)(2,1)} %get-tuple-element.60), channel_id=1, source_target_pairs={{0,1},{1,2},{2,3},{3,0},{4,5},{5,6},{6,7},{7,4},{8,9},{9,10},{10,1... | collective-permute-start | bytes 393224 | tf_op jit(solution)/shard_map/ppermute | solution.py:255
  176.1 22.0 %collective-permute-start.17 = (bf16[256,256]{1,0:T(8,128)(2,1)}, bf16[256,256]{1,0:T(8,128)(2,1)S(1)}, u32[]{:S(2)}, u32[]{:S(2)}) collective-permute-start(bf16[256,256]{1,0:T(8,128)(2,1)} %get-tuple-element.54), channel_id=1, source_target_pairs={{0,3},{1,0},{2,1},{3,2},{4,7},{5,4},{6,5},{7,6},{8,11},{9,8},{10,9... | collective-permute-start | bytes 393224 | tf_op jit(solution)/shard_map/ppermute | solution.py:255
  177.9 5.9 %copy-start.19 = (bf16[8,256,256]{2,1,0:T(8,128)(2,1)}, bf16[8,256,256]{2,1,0:T(8,128)(2,1)S(1)}, u32[]{:S(2)}) copy-start(bf16[8,256,256]{2,1,0:T(8,128)(2,1)S(1)} %collective-permute-done.12.refs_8_) | copy-start | bytes 3145732
  177.9 15.0 %copy-start.20 = (bf16[256,256]{1,0:T(8,128)(2,1)S(1)}, bf16[256,256]{1,0:T(8,128)(2,1)}, u32[]{:S(2)}) copy-start(bf16[256,256]{1,0:T(8,128)(2,1)} %get-tuple-element.56) | copy-start | bytes 393220
  177.9 23.6 %collective-permute-start.18 = (bf16[256,256]{1,0:T(8,128)(2,1)}, bf16[256,256]{1,0:T(8,128)(2,1)S(1)}, u32[]{:S(2)}, u32[]{:S(2)}) collective-permute-start(bf16[256,256]{1,0:T(8,128)(2,1)} %get-tuple-element.55), channel_id=1, source_target_pairs={{0,2},{1,3},{2,0},{3,1},{4,6},{5,7},{6,4},{7,5},{8,10},{9,11},{10,... | collective-permute-start | bytes 393224 | tf_op jit(solution)/shard_map/ppermute | solution.py:255
  192.9 6.7 %copy-start.10 = (bf16[256,256]{1,0:T(8,128)(2,1)}, bf16[256,256]{1,0:T(8,128)(2,1)S(1)}, u32[]{:S(2)}) copy-start(bf16[256,256]{1,0:T(8,128)(2,1)S(1)} %collective-permute-done.21.refs_1_) | copy-start | bytes 393220
  192.9 8.6 %collective-permute-start.19 = (bf16[256,256]{1,0:T(8,128)(2,1)S(1)}, bf16[256,256]{1,0:T(8,128)(2,1)S(1)}, u32[]{:S(2)}, u32[]{:S(2)}) collective-permute-start(bf16[256,256]{1,0:T(8,128)(2,1)S(1)} %copy-done.20), channel_id=1, source_target_pairs={{0,1},{1,2},{2,3},{3,0},{4,5},{5,6},{6,7},{7,4},{8,9},{9,10},{10,1... | collective-permute-start | bytes 393224 | tf_op jit(solution)/shard_map/ppermute | solution.py:255
  193.0 6.6 %copy-start.11 = (bf16[256,256]{1,0:T(8,128)(2,1)}, bf16[256,256]{1,0:T(8,128)(2,1)S(1)}, u32[]{:S(2)}) copy-start(bf16[256,256]{1,0:T(8,128)(2,1)S(1)} %collective-permute-done.22.refs_2_) | copy-start | bytes 393220
  193.0 11.0 %collective-permute-start.13 = (bf16[256,256]{1,0:T(8,128)(2,1)}, bf16[256,256]{1,0:T(8,128)(2,1)S(1)}, u32[]{:S(2)}, u32[]{:S(2)}) collective-permute-start(bf16[256,256]{1,0:T(8,128)(2,1)} %get-tuple-element.50), channel_id=1, source_target_pairs={{0,3},{1,0},{2,1},{3,2},{4,7},{5,4},{6,5},{7,6},{8,11},{9,8},{10,9... | collective-permute-start | bytes 393224 | tf_op jit(solution)/shard_map/ppermute | solution.py:255
  197.1 2.5 %copy-start.12 = (bf16[256,256]{1,0:T(8,128)(2,1)}, bf16[256,256]{1,0:T(8,128)(2,1)S(1)}, u32[]{:S(2)}) copy-start(bf16[256,256]{1,0:T(8,128)(2,1)S(1)} %collective-permute-done.23.refs_3_) | copy-start | bytes 393220
  197.1 9.1 %collective-permute-start.14 = (bf16[256,256]{1,0:T(8,128)(2,1)}, bf16[256,256]{1,0:T(8,128)(2,1)S(1)}, u32[]{:S(2)}, u32[]{:S(2)}) collective-permute-start(bf16[256,256]{1,0:T(8,128)(2,1)} %get-tuple-element.51), channel_id=1, source_target_pairs={{0,2},{1,3},{2,0},{3,1},{4,6},{5,7},{6,4},{7,5},{8,10},{9,11},{10,... | collective-permute-start | bytes 393224 | tf_op jit(solution)/shard_map/ppermute | solution.py:255
  198.1 3.4 %copy-start.13 = (bf16[256,256]{1,0:T(8,128)(2,1)}, bf16[256,256]{1,0:T(8,128)(2,1)S(1)}, u32[]{:S(2)}) copy-start(bf16[256,256]{1,0:T(8,128)(2,1)S(1)} %collective-permute-done.17.refs_1_) | copy-start | bytes 393220
  198.1 8.1 %collective-permute-start.15 = (bf16[256,256]{1,0:T(8,128)(2,1)}, bf16[256,256]{1,0:T(8,128)(2,1)S(1)}, u32[]{:S(2)}, u32[]{:S(2)}) collective-permute-start(bf16[256,256]{1,0:T(8,128)(2,1)} %get-tuple-element.52), channel_id=1, source_target_pairs={{0,1},{1,2},{2,3},{3,0},{4,5},{5,6},{6,7},{7,4},{8,9},{9,10},{10,1... | collective-permute-start | bytes 393224 | tf_op jit(solution)/shard_map/ppermute | solution.py:255
  201.4 0.7 copy-start.14
  201.4 0.7 copy-start.17
  204.0 2.2 %copy-start.15 = (bf16[256,256]{1,0:T(8,128)(2,1)}, bf16[256,256]{1,0:T(8,128)(2,1)S(1)}, u32[]{:S(2)}) copy-start(bf16[256,256]{1,0:T(8,128)(2,1)S(1)} %collective-permute-done.13.refs_1_) | copy-start | bytes 393220
  206.2 0.7 copy-start.16
  206.2 0.7 copy-start.18

commit v2 on v1

--- a/solution.py
+++ b/solution.py
@@ -10,7 +10,8 @@
 
 HD = 128
 TILE = 128
-CHUNKS = ((2, 1), (2, 0), (2, 1))
+CHUNKS = ((3, 0), (3, 0))
+RELAYED = 1
 SCALE = math.log2(math.e) / math.sqrt(HD)
 ANY = pl.BlockSpec(memory_space=pl.ANY)
 SMEM = pl.BlockSpec(memory_space=pltpu.SMEM)
@@ -141,9 +142,10 @@
     )(*arrays)
 
 
-def attend_body(ways, chunk, noise, mask, *refs):
-    pieces, asks, prior, outs = refs[:ways], refs[ways : 2 * ways], refs[2 * ways], refs[-ways:]
-    rows = prior.shape[1]
+def attend_body(ways, chunk, sums, noise, mask, *refs):
+    pieces, asks, outs = refs[:ways], refs[ways : 2 * ways], refs[-ways:]
+    priors = refs[2 * ways : 2 * ways + sums]
+    rows = priors[0].shape[1]
     per = rows // TILE
     tiles = ways * per
     me, group = lax.axis_index("head"), lax.axis_index("group")
@@ -154,15 +156,16 @@
     first = [lax.rem(me + ways - r, ways) * per for r in range(ways)]
     before = [lax.rem(me + moved + ways - r, ways) * per for r in range(ways)]
     lane = lax.broadcasted_iota(jnp.int32, (1, rows), 1) // TILE
-    context = [(prior.at[2 * p], prior.at[2 * p + 1], before[p], see) for p in range(ways)]
-    context += [(pieces[p].at[0], pieces[p].at[1], tiles + first[p], 1) for p in range(ways)]
+    past = [functools.reduce(jnp.add, [prior[i] for prior in priors]) for i in range(2 * ways)]
+    context = [(past[2 * p], past[2 * p + 1], before[p], see) for p in range(ways)]
+    context += [(pieces[p][0], pieces[p][1], tiles + first[p], 1) for p in range(ways)]
 
     def score(r):
         query = asks[r][...]
         scores = []
         for key, _, tile, seen in context:
             s = lax.dot_general(
-                query, key[...], (((1,), (1,)), ((), ())), preferred_element_type=jnp.float32
+                query, key, (((1,), (1,)), ((), ())), preferred_element_type=jnp.float32
             )
             bands = []
             for a in range(per):
@@ -189,25 +192,25 @@
             weights = jnp.exp2((s - top) * SCALE)
             total = total + weights
             result = result + jnp.dot(
-                weights.astype(jnp.bfloat16), value[...], preferred_element_type=jnp.float32
+                weights.astype(jnp.bfloat16), value, preferred_element_type=jnp.float32
             )
         total = jnp.sum(total, axis=1, keepdims=True)
         outs[r][...] = (result / total).astype(jnp.bfloat16)
 
 
-def attend(noise_level, tile_mask, pieces, asks, prior, chunk, start, gates):
+def attend(noise_level, tile_mask, pieces, asks, priors, chunk, start, gates):
     ways = len(pieces)
-    rows, wide = prior.shape[1:]
+    rows, wide = priors[0].shape[1:]
     heads, skip = wide // HD, start // HD
     pairs = heads * ways * rows * 2 * ways * rows
     return pl.pallas_call(
-        functools.partial(attend_body, ways, chunk),
+        functools.partial(attend_body, ways, chunk, len(priors)),
         grid=(heads,),
         out_shape=[jax.ShapeDtypeStruct((rows, wide), jnp.bfloat16)] * ways,
         in_specs=[SMEM, SMEM]
         + [pl.BlockSpec((2, rows, HD), lambda h: (0, 0, h))] * ways
         + [pl.BlockSpec((rows, HD), lambda h: (0, h + skip))] * ways
-        + [pl.BlockSpec((2 * ways, rows, HD), lambda h: (0, 0, h))]
+        + [pl.BlockSpec((2 * ways, rows, HD), lambda h: (0, 0, h))] * len(priors)
         + [ANY] * len(gates),
         out_specs=[pl.BlockSpec((rows, HD), lambda h: (0, h))] * ways,
         compiler_params=pltpu.CompilerParams(vmem_limit_bytes=VMEM_LIMIT),
@@ -215,7 +218,7 @@
             flops=8 * pairs * HD, bytes_accessed=12 * ways * rows * wide, transcendentals=pairs
         ),
         name="attend",
-    )(noise_level, tile_mask, *pieces, *asks, prior, *gates)
+    )(noise_level, tile_mask, *pieces, *asks, *priors, *gates)
 
 
 def place_body(ways, width, chunk, start, *refs):
@@ -255,14 +258,23 @@
     return lax.ppermute(block, "head", [(i, (i + distance) % ways) for i in range(ways)])
 
 
-def onward(block, chunk):
+def onward(block, chunk, relayed):
     count, ways = lax.axis_size("group"), lax.axis_size("head")
-    pairs = []
+    half = count // 2
+    pairs, last = [], []
     for group in range(count - 1):
-        back = chunk[1] if group + 1 == count // 2 else 0
         for i in range(ways):
-            pairs.append((group * ways + i, (group + 1) * ways + (i - back) % ways))
-    return lax.ppermute(block, ("group", "head"), pairs)
+            there = (group + 1) * ways + i
+            if group + 1 == half:
+                there = half * ways + (i - chunk[1]) % ways
+                if relayed:
+                    last.append((i, there))
+                    there = i
+            pairs.append((group * ways + i, there))
+    block = lax.ppermute(block, ("group", "head"), pairs)
+    if not relayed:
+        return [block]
+    return [block, lax.ppermute(block, ("group", "head"), last)]
 
 
 def shards(queries, keys, values, noise_level, tile_mask):
@@ -278,8 +290,10 @@
     gathered = []
     for part in pieces:
         gathered.append(gather(part, gathered[-1:]))
-    priors = [onward(block, chunk) for block, chunk in zip(gathered, CHUNKS)]
-    gates = [touch(asks)]
+    priors = [
+        onward(block, chunk, j < RELAYED) for j, (block, chunk) in enumerate(zip(gathered, CHUNKS))
+    ]
+    gates = [touch([prior[0] for prior in priors[RELAYED:]])]
     out = None
     for j, (chunk, start, _) in enumerate(spans()):
         result = attend(noise_level, tile_mask, pieces[j], asks, priors[j], chunk, start, gates)

time: 209 us -> 191 us (0.914)
  starting transfers between devices: 73 us -> 43.1 us
  waiting for transfers between devices: 89.8 us -> 103 us
  Pallas kernels: 44.1 us -> 38.7 us
  local copies, waits for them, and re-layouts: 1.45 us -> 5.6 us
    ppermute x21 -> x15, starting transfers between devices: 64.6 us -> 37.4 us  [turn(): lax.ppermute(block, 'head', [(i, (i + distance) % ways) for i in range(wa...]
    ppermute x3, waiting for transfers between devices: 26.8 us -> 47.3 us  [the longest x2 39.2 us: onward(): block = lax.ppermute(block, ('group', 'head'), pairs)]
    ppermute x21 -> x15, waiting for transfers between devices: 63 us -> 55.7 us  [turn(): lax.ppermute(block, 'head', [(i, (i + distance) % ways) for i in range(wa...]
    unnamed x42 -> x34, local copies, waits for them, and re-layouts: 1.45 us -> 5.6 us
    ppermute x3, starting transfers between devices: 8.42 us -> 5.68 us  [the longest x2 4.4 us: onward(): block = lax.ppermute(block, ('group', 'head'), pairs)]
    pallas_call x3 -> x2, Pallas kernels: 27.1 us -> 25 us  [attend(): pl.pallas_call(functools.partial(attend_body, ways, chunk, len(priors)),...]
    pallas_call x3 -> x2, Pallas kernels: 6.07 us -> 4.47 us  [gather(): pl.pallas_call(functools.partial(gather_body, ways), out_shape=jax.ShapeD...]
    pallas_call x3 -> x2, Pallas kernels: 5.45 us -> 3.92 us  [place(): pl.pallas_call(functools.partial(place_body, ways, width, chunk, start),...]
  transfers between devices with their start and end apart: 24 -> 18, of which waited for: 8 -> 7; matrix products, arithmetic and copies ran while one was open for 0% -> 0% of each run, Pallas kernels for 18% -> 10%
where the time goes in v2:
time: 191 us
  waiting for transfers between devices  103 us (54%)
  starting transfers between devices  43.1 us (23%)
  Pallas kernels  38.7 us (20%)
  local copies, waits for them, and re-layouts  5.6 us (3%)
    ppermute x15, waiting for transfers between devices, turn(): lax.ppermute(block, 'head', [(i, (i + distance) % ways) for i in range(wa...  55.7 us
    ppermute x2, waiting for transfers between devices, onward(): block = lax.ppermute(block, ('group', 'head'), pairs)  39.2 us
    ppermute x15, starting transfers between devices, turn(): lax.ppermute(block, 'head', [(i, (i + distance) % ways) for i in range(wa...  37.4 us
    pallas_call x2, Pallas kernels, attend(): pl.pallas_call(functools.partial(attend_body, ways, chunk, len(priors)),...  25 us
    ppermute x1, waiting for transfers between devices, onward(): return [block, lax.ppermute(block, ('group', 'head'), last)]  8.06 us
    unnamed x34, local copies, waits for them, and re-layouts  5.6 us
    pallas_call x1, Pallas kernels, pack(): pl.pallas_call(functools.partial(pack_body, ways, width, order), out_shap...  4.77 us
    pallas_call x2, Pallas kernels, gather(): pl.pallas_call(functools.partial(gather_body, ways), out_shape=jax.ShapeD...  4.47 us
  transfers between devices with their start and end apart: 18, of which 7 were waited for; matrix products, arithmetic and copies ran while one was open for 0% of the time, Pallas kernels for 10%

profile of v2, /device:TPU:32, one launch (start us, length us, event | category | flops | bytes accessed | tf_op | source)
XLA Modules:
  0.0 190.8 jit_solution(7640717646687006856)
XLA Ops:
  0.0 4.8 %pack.1 = (bf16[2,256,384]{2,1,0:T(8,128)(2,1)}, bf16[2,256,384]{2,1,0:T(8,128)(2,1)}, bf16[2,256,384]{2,1,0:T(8,128)(2,1)}, bf16[2,256,384]{2,1,0:T(8,128)(2,1)...) custom-call(bf16[256,3072]{1,0:T(8,128)(2,1)} %refs_0_.1, ...), custom_call_target="tpu_custom_call" | custom-call | tf_op jit(solution)/shard_map/pack/pallas_call | solution.py:99
  4.8 3.3 %collective-permute-start.6 = (bf16[2,256,384]{2,1,0:T(8,128)(2,1)}, bf16[2,256,384]{2,1,0:T(8,128)(2,1)S(1)}, u32[]{:S(2)}, u32[]{:S(2)}) collective-permute-start(bf16[2,256,384]{2,1,0:T(8,128)(2,1)} %get-tuple-element.34), channel_id=1, source_target_pairs={{0,1},{1,2},{2,3},{3,0},{4,5},{5,6},{6,7},{7,4},{8,9},{9,10},{10,1... | collective-permute-start | bytes 1179656 | tf_op jit(solution)/shard_map/ppermute | solution.py:258
  8.1 4.5 %collective-permute-start.7 = (bf16[2,256,384]{2,1,0:T(8,128)(2,1)}, bf16[2,256,384]{2,1,0:T(8,128)(2,1)S(1)}, u32[]{:S(2)}, u32[]{:S(2)}) collective-permute-start(bf16[2,256,384]{2,1,0:T(8,128)(2,1)} %get-tuple-element.35), channel_id=1, source_target_pairs={{0,2},{1,3},{2,0},{3,1},{4,6},{5,7},{6,4},{7,5},{8,10},{9,11},{10,... | collective-permute-start | bytes 1179656 | tf_op jit(solution)/shard_map/ppermute | solution.py:258
  12.6 2.7 %collective-permute-start.8 = (bf16[2,256,384]{2,1,0:T(8,128)(2,1)}, bf16[2,256,384]{2,1,0:T(8,128)(2,1)S(1)}, u32[]{:S(2)}, u32[]{:S(2)}) collective-permute-start(bf16[2,256,384]{2,1,0:T(8,128)(2,1)} %get-tuple-element.36), channel_id=1, source_target_pairs={{0,3},{1,0},{2,1},{3,2},{4,7},{5,4},{6,5},{7,6},{8,11},{9,8},{10,9... | collective-permute-start | bytes 1179656 | tf_op jit(solution)/shard_map/ppermute | solution.py:258
  15.3 0.3 collective-permute-start
  15.5 2.1 %collective-permute-start.1 = (bf16[2,256,384]{2,1,0:T(8,128)(2,1)}, bf16[2,256,384]{2,1,0:T(8,128)(2,1)S(1)}, u32[]{:S(2)}, u32[]{:S(2)}) collective-permute-start(bf16[2,256,384]{2,1,0:T(8,128)(2,1)} %get-tuple-element.27), channel_id=1, source_target_pairs={{0,2},{1,3},{2,0},{3,1},{4,6},{5,7},{6,4},{7,5},{8,10},{9,11},{10,... | collective-permute-start | bytes 1179656 | tf_op jit(solution)/shard_map/ppermute | solution.py:258
  17.6 23.2 %collective-permute-done.6.refs_1_ = bf16[2,256,384]{2,1,0:T(8,128)(2,1)S(1)} collective-permute-done((bf16[2,256,384]{2,1,0:T(8,128)(2,1)}, bf16[2,256,384]{2,1,0:T(8,128)(2,1)S(1)}, u32[]{:S(2)}, u32[]{:S(2)}) %collective-permute-start.6) | collective-permute-done | bytes 393248 | tf_op jit(solution)/shard_map/ppermute | solution.py:258
  40.8 3.0 %collective-permute-start.2 = (bf16[2,256,384]{2,1,0:T(8,128)(2,1)}, bf16[2,256,384]{2,1,0:T(8,128)(2,1)S(1)}, u32[]{:S(2)}, u32[]{:S(2)}) collective-permute-start(bf16[2,256,384]{2,1,0:T(8,128)(2,1)} %get-tuple-element.28), channel_id=1, source_target_pairs={{0,3},{1,0},{2,1},{3,2},{4,7},{5,4},{6,5},{7,6},{8,11},{9,8},{10,9... | collective-permute-start | bytes 1179656 | tf_op jit(solution)/shard_map/ppermute | solution.py:258
  43.8 0.0 collective-permute-done.7.refs_2_
  43.8 0.0 collective-permute-done.8.refs_3_
  43.8 0.7 copy-done.3
  44.6 0.2 copy-done.4
  44.7 2.2 %gather.2.refs_4_ = bf16[8,256,384]{2,1,0:T(8,128)(2,1)} custom-call(bf16[2,256,384]{2,1,0:T(8,128)(2,1)} %get-tuple-element.33.refs_0_, bf16[2,256,384]{2,1,0:T(8,128)(2,1)} %copy-done.2, bf16[2,256,384]{2,1,0:T(8,128)(2,1)} %copy-done.3, bf16[2,256,384]{2,1,0:T(8,128)(2,1)} %copy-done.4), custom_call_target="tpu_custom_call" | custom-call | tf_op jit(solution)/shard_map/gather/pallas_call | solution.py:119
  46.9 2.5 %collective-permute-start.13 = (bf16[8,256,384]{2,1,0:T(8,128)(2,1)}, bf16[8,256,384]{2,1,0:T(8,128)(2,1)}, u32[]{:S(2)}, u32[]{:S(2)}) collective-permute-start(bf16[8,256,384]{2,1,0:T(8,128)(2,1)} %gather.2.refs_4_), channel_id=1, source_target_pairs={{0,4},{1,5},{2,6},{3,7},{4,8},{5,9},{6,10},{7,11},{8,12},{9,13},{1... | collective-permute-start | bytes 4718600 | tf_op jit(solution)/shard_map/ppermute | solution.py:274
  49.4 19.7 %collective-permute-done.refs_1_ = bf16[2,256,384]{2,1,0:T(8,128)(2,1)S(1)} collective-permute-done((bf16[2,256,384]{2,1,0:T(8,128)(2,1)}, bf16[2,256,384]{2,1,0:T(8,128)(2,1)S(1)}, u32[]{:S(2)}, u32[]{:S(2)}) %collective-permute-start) | collective-permute-done | bytes 393248 | tf_op jit(solution)/shard_map/ppermute | solution.py:258
  69.1 0.0 collective-permute-done.1.refs_2_
  69.2 0.7 copy-done
  69.9 0.1 copy-done.1
  70.0 0.1 copy-done.5
  70.2 2.3 %gather.3 = bf16[8,256,384]{2,1,0:T(8,128)(2,1)} custom-call(bf16[2,256,384]{2,1,0:T(8,128)(2,1)} %get-tuple-element.25.refs_0_, bf16[2,256,384]{2,1,0:T(8,128)(2,1)} %copy-done, bf16[2,256,384]{2,1,0:T(8,128)(2,1)} %copy-done.1, bf16[2,256,384]{2,1,0:T(8,128)(2,1)} %copy-done.5, bf16[8,256,384]{2,1,0:T(8,128)(2,1)} %gather.2.refs_4_), custom_call_target="tpu_custom_call" | custom-call | tf_op jit(solution)/shard_map/gather/pallas_call | solution.py:119
  72.4 1.9 %collective-permute-start.9 = (bf16[8,256,384]{2,1,0:T(8,128)(2,1)}, bf16[8,256,384]{2,1,0:T(8,128)(2,1)S(1)}, u32[]{:S(2)}, u32[]{:S(2)}) collective-permute-start(bf16[8,256,384]{2,1,0:T(8,128)(2,1)} %gather.3), channel_id=1, source_target_pairs={{0,4},{1,5},{2,6},{3,7},{4,8},{5,9},{6,10},{7,11},{8,12},{9,13},{1... | collective-permute-start | bytes 4718600 | tf_op jit(solution)/shard_map/ppermute | solution.py:274
  74.4 2.4 %collective-permute-start.3 = (bf16[256,768]{1,0:T(8,128)(2,1)}, bf16[256,768]{1,0:T(8,128)(2,1)}, u32[]{:S(2)}, u32[]{:S(2)}) collective-permute-start(bf16[256,768]{1,0:T(8,128)(2,1)} %get-tuple-element.30), channel_id=1, source_target_pairs={{0,1},{1,2},{2,3},{3,0},{4,5},{5,6},{6,7},{7,4},{8,9},{9,10},{10,1... | collective-permute-start | bytes 1179656 | tf_op jit(solution)/shard_map/ppermute | solution.py:258
  76.7 1.8 collective-permute-start.4
  78.6 3.5 %collective-permute-start.5 = (bf16[256,768]{1,0:T(8,128)(2,1)S(1)}, bf16[256,768]{1,0:T(8,128)(2,1)}, u32[]{:S(2)}, u32[]{:S(2)}) collective-permute-start(bf16[256,768]{1,0:T(8,128)(2,1)S(1)} %copy-done.14), channel_id=1, source_target_pairs={{0,3},{1,0},{2,1},{3,2},{4,7},{5,4},{6,5},{7,6},{8,11},{9,8},{10,9... | collective-permute-start | bytes 1179656 | tf_op jit(solution)/shard_map/ppermute | solution.py:258
  82.1 0.0 collective-permute-done.13.refs_8_
  82.1 1.3 collective-permute-start.14
  83.4 39.2 %collective-permute-done.9.refs_0_.refs_8_ = bf16[8,256,384]{2,1,0:T(8,128)(2,1)S(1)} collective-permute-done((bf16[8,256,384]{2,1,0:T(8,128)(2,1)}, bf16[8,256,384]{2,1,0:T(8,128)(2,1)S(1)}, u32[]{:S(2)}, u32[]{:S(2)}) %collective-permute-start.9) | collective-permute-done | bytes 1572896 | tf_op jit(solution)/shard_map/ppermute | solution.py:274
  122.6 1.1 copy-done.12
  123.8 0.5 touch.1.refs_9_.refs_10_
  124.3 0.0 collective-permute-done.3.refs_5_
  124.3 8.1 %collective-permute-done.14.refs_9_ = bf16[8,256,384]{2,1,0:T(8,128)(2,1)S(1)} collective-permute-done((bf16[8,256,384]{2,1,0:T(8,128)(2,1)}, bf16[8,256,384]{2,1,0:T(8,128)(2,1)S(1)}, u32[]{:S(2)}, u32[]{:S(2)}) %collective-permute-start.14) | collective-permute-done | bytes 1572896 | tf_op jit(solution)/shard_map/ppermute | solution.py:277
  132.4 1.2 copy-done.13
  133.5 12.7 %attend.3 = (bf16[256,384]{1,0:T(8,128)(2,1)}, bf16[256,384]{1,0:T(8,128)(2,1)}, bf16[256,384]{1,0:T(8,128)(2,1)}, bf16[256,384]{1,0:T(8,128)(2,1)}) custom-call(s32[64]{0:T(128)} %noise.3, s32[1,8,16]{2,1,0:T(8,128)} %mask.3, bf16[2,256,384]{2,1,0:T(8,128)(2,1)} %get-tuple-element.33.refs_0_, bf16[2,256,384]{2,1,0:T(8,128)(2,1)} %copy-done.2, ...), custom_call_target="tpu_custom_call" | custom-call | flops 6442450944 | bytes 4718592 | tf_op jit(solution)/shard_map/attend/pallas_call | solution.py:206
  146.3 3.4 %collective-permute-start.15 = (bf16[256,384]{1,0:T(8,128)(2,1)}, bf16[256,384]{1,0:T(8,128)(2,1)S(1)}, u32[]{:S(2)}, u32[]{:S(2)}) collective-permute-start(bf16[256,384]{1,0:T(8,128)(2,1)} %get-tuple-element.42), channel_id=1, source_target_pairs={{0,3},{1,0},{2,1},{3,2},{4,7},{5,4},{6,5},{7,6},{8,11},{9,8},{10,9... | collective-permute-start | bytes 589832 | tf_op jit(solution)/shard_map/ppermute | solution.py:258
  149.6 12.3 %attend.2 = (bf16[256,384]{1,0:T(8,128)(2,1)}, bf16[256,384]{1,0:T(8,128)(2,1)}, bf16[256,384]{1,0:T(8,128)(2,1)}, bf16[256,384]{1,0:T(8,128)(2,1)}) custom-call(s32[64]{0:T(128)} %noise.3, s32[1,8,16]{2,1,0:T(8,128)} %mask.3, bf16[2,256,384]{2,1,0:T(8,128)(2,1)} %get-tuple-element.25.refs_0_, bf16[2,256,384]{2,1,0:T(8,128)(2,1)} %copy-done, ...), custom_call_target="tpu_custom_call" | custom-call | flops 6442450944 | bytes 4718592 | tf_op jit(solution)/shard_map/attend/pallas_call | solution.py:206
  162.0 2.3 %collective-permute-start.10 = (bf16[256,384]{1,0:T(8,128)(2,1)}, bf16[256,384]{1,0:T(8,128)(2,1)S(1)}, u32[]{:S(2)}, u32[]{:S(2)}) collective-permute-start(bf16[256,384]{1,0:T(8,128)(2,1)} %get-tuple-element.38), channel_id=1, source_target_pairs={{0,3},{1,0},{2,1},{3,2},{4,7},{5,4},{6,5},{7,6},{8,11},{9,8},{10,9... | collective-permute-start | bytes 589832 | tf_op jit(solution)/shard_map/ppermute | solution.py:258
  164.3 1.6 collective-permute-start.16
  165.9 2.8 %collective-permute-start.17 = (bf16[256,384]{1,0:T(8,128)(2,1)S(1)}, bf16[256,384]{1,0:T(8,128)(2,1)S(1)}, u32[]{:S(2)}, u32[]{:S(2)}) collective-permute-start(bf16[256,384]{1,0:T(8,128)(2,1)S(1)} %copy-done.15), channel_id=1, source_target_pairs={{0,1},{1,2},{2,3},{3,0},{4,5},{5,6},{6,7},{7,4},{8,9},{9,10},{10,1... | collective-permute-start | bytes 589832 | tf_op jit(solution)/shard_map/ppermute | solution.py:258
  168.7 2.2 %collective-permute-start.11 = (bf16[256,384]{1,0:T(8,128)(2,1)}, bf16[256,384]{1,0:T(8,128)(2,1)S(1)}, u32[]{:S(2)}, u32[]{:S(2)}) collective-permute-start(bf16[256,384]{1,0:T(8,128)(2,1)} %get-tuple-element.39), channel_id=1, source_target_pairs={{0,2},{1,3},{2,0},{3,1},{4,6},{5,7},{6,4},{7,5},{8,10},{9,11},{10,... | collective-permute-start | bytes 589832 | tf_op jit(solution)/shard_map/ppermute | solution.py:258
  170.9 1.5 collective-permute-start.12
  172.4 2.0 %collective-permute-done.16.refs_2_ = bf16[256,384]{1,0:T(8,128)(2,1)S(1)} collective-permute-done((bf16[256,384]{1,0:T(8,128)(2,1)S(1)}, bf16[256,384]{1,0:T(8,128)(2,1)S(1)}, u32[]{:S(2)}, u32[]{:S(2)}) %collective-permute-start.16) | collective-permute-done | bytes 196640 | tf_op jit(solution)/shard_map/ppermute | solution.py:258
  174.4 5.0 %collective-permute-done.17.refs_3_ = bf16[256,384]{1,0:T(8,128)(2,1)S(1)} collective-permute-done((bf16[256,384]{1,0:T(8,128)(2,1)S(1)}, bf16[256,384]{1,0:T(8,128)(2,1)S(1)}, u32[]{:S(2)}, u32[]{:S(2)}) %collective-permute-start.17) | collective-permute-done | bytes 196640 | tf_op jit(solution)/shard_map/ppermute | solution.py:258
  179.4 0.7 copy-done.8
  180.1 2.0 %place.2.refs_4_ = bf16[256,3072]{1,0:T(8,128)(2,1)} custom-call(bf16[256,384]{1,0:T(8,128)(2,1)} %get-tuple-element.41.refs_0_, bf16[256,384]{1,0:T(8,128)(2,1)} %copy-done.6, bf16[256,384]{1,0:T(8,128)(2,1)} %copy-done.7, bf16[256,384]{1,0:T(8,128)(2,1)} %copy-done.8), custom_call_target="tpu_custom_call" | custom-call | tf_op jit(solution)/shard_map/place/pallas_call | solution.py:242
  182.0 0.0 collective-permute-done.11.refs_2_
  182.1 5.9 %collective-permute-done.12.refs_3_ = bf16[256,384]{1,0:T(8,128)(2,1)S(1)} collective-permute-done((bf16[256,384]{1,0:T(8,128)(2,1)}, bf16[256,384]{1,0:T(8,128)(2,1)S(1)}, u32[]{:S(2)}, u32[]{:S(2)}) %collective-permute-start.12) | collective-permute-done | bytes 196640 | tf_op jit(solution)/shard_map/ppermute | solution.py:258
  187.9 0.7 copy-done.11
  188.6 2.0 %place.3 = bf16[256,3072]{1,0:T(8,128)(2,1)} custom-call(bf16[256,384]{1,0:T(8,128)(2,1)} %get-tuple-element.37.refs_0_, bf16[256,384]{1,0:T(8,128)(2,1)} %copy-done.9, bf16[256,384]{1,0:T(8,128)(2,1)} %copy-done.10, bf16[256,384]{1,0:T(8,128)(2,1)} %copy-done.11, bf16[256,3072]{1,0:T(8,128)(2,1)} %place.2.refs_4_), custom_call_target="tpu_custom_call", output_to_operand_aliasing={{}: (4, {})} | custom-call | tf_op jit(solution)/shard_map/place/pallas_call | solution.py:242
  (30 shorter events, 0.1 us)
Async XLA Ops:
  4.8 36.0 %collective-permute-start.6 = (bf16[2,256,384]{2,1,0:T(8,128)(2,1)}, bf16[2,256,384]{2,1,0:T(8,128)(2,1)S(1)}, u32[]{:S(2)}, u32[]{:S(2)}) collective-permute-start(bf16[2,256,384]{2,1,0:T(8,128)(2,1)} %get-tuple-element.34), channel_id=1, source_target_pairs={{0,1},{1,2},{2,3},{3,0},{4,5},{5,6},{6,7},{7,4},{8,9},{9,10},{10,1... | collective-permute-start | bytes 1179656 | tf_op jit(solution)/shard_map/ppermute | solution.py:258
  8.1 35.7 %collective-permute-start.7 = (bf16[2,256,384]{2,1,0:T(8,128)(2,1)}, bf16[2,256,384]{2,1,0:T(8,128)(2,1)S(1)}, u32[]{:S(2)}, u32[]{:S(2)}) collective-permute-start(bf16[2,256,384]{2,1,0:T(8,128)(2,1)} %get-tuple-element.35), channel_id=1, source_target_pairs={{0,2},{1,3},{2,0},{3,1},{4,6},{5,7},{6,4},{7,5},{8,10},{9,11},{10,... | collective-permute-start | bytes 1179656 | tf_op jit(solution)/shard_map/ppermute | solution.py:258
  12.6 31.2 %collective-permute-start.8 = (bf16[2,256,384]{2,1,0:T(8,128)(2,1)}, bf16[2,256,384]{2,1,0:T(8,128)(2,1)S(1)}, u32[]{:S(2)}, u32[]{:S(2)}) collective-permute-start(bf16[2,256,384]{2,1,0:T(8,128)(2,1)} %get-tuple-element.36), channel_id=1, source_target_pairs={{0,3},{1,0},{2,1},{3,2},{4,7},{5,4},{6,5},{7,6},{8,11},{9,8},{10,9... | collective-permute-start | bytes 1179656 | tf_op jit(solution)/shard_map/ppermute | solution.py:258
  15.3 53.9 %collective-permute-start = (bf16[2,256,384]{2,1,0:T(8,128)(2,1)}, bf16[2,256,384]{2,1,0:T(8,128)(2,1)S(1)}, u32[]{:S(2)}, u32[]{:S(2)}) collective-permute-start(bf16[2,256,384]{2,1,0:T(8,128)(2,1)} %get-tuple-element.26), channel_id=1, source_target_pairs={{0,1},{1,2},{2,3},{3,0},{4,5},{5,6},{6,7},{7,4},{8,9},{9,10},{10,1... | collective-permute-start | bytes 1179656 | tf_op jit(solution)/shard_map/ppermute | solution.py:258
  15.5 53.6 %collective-permute-start.1 = (bf16[2,256,384]{2,1,0:T(8,128)(2,1)}, bf16[2,256,384]{2,1,0:T(8,128)(2,1)S(1)}, u32[]{:S(2)}, u32[]{:S(2)}) collective-permute-start(bf16[2,256,384]{2,1,0:T(8,128)(2,1)} %get-tuple-element.27), channel_id=1, source_target_pairs={{0,2},{1,3},{2,0},{3,1},{4,6},{5,7},{6,4},{7,5},{8,10},{9,11},{10,... | collective-permute-start | bytes 1179656 | tf_op jit(solution)/shard_map/ppermute | solution.py:258
  40.8 3.0 %copy-start.2 = (bf16[2,256,384]{2,1,0:T(8,128)(2,1)}, bf16[2,256,384]{2,1,0:T(8,128)(2,1)S(1)}, u32[]{:S(2)}) copy-start(bf16[2,256,384]{2,1,0:T(8,128)(2,1)S(1)} %collective-permute-done.6.refs_1_) | copy-start | bytes 1179652
  40.8 28.3 %collective-permute-start.2 = (bf16[2,256,384]{2,1,0:T(8,128)(2,1)}, bf16[2,256,384]{2,1,0:T(8,128)(2,1)S(1)}, u32[]{:S(2)}, u32[]{:S(2)}) collective-permute-start(bf16[2,256,384]{2,1,0:T(8,128)(2,1)} %get-tuple-element.28), channel_id=1, source_target_pairs={{0,3},{1,0},{2,1},{3,2},{4,7},{5,4},{6,5},{7,6},{8,11},{9,8},{10,9... | collective-permute-start | bytes 1179656 | tf_op jit(solution)/shard_map/ppermute | solution.py:258
  43.8 0.7 copy-start.3
  43.8 0.9 copy-start.4
  46.9 35.2 %collective-permute-start.13 = (bf16[8,256,384]{2,1,0:T(8,128)(2,1)}, bf16[8,256,384]{2,1,0:T(8,128)(2,1)}, u32[]{:S(2)}, u32[]{:S(2)}) collective-permute-start(bf16[8,256,384]{2,1,0:T(8,128)(2,1)} %gather.2.refs_4_), channel_id=1, source_target_pairs={{0,4},{1,5},{2,6},{3,7},{4,8},{5,9},{6,10},{7,11},{8,12},{9,13},{1... | collective-permute-start | bytes 4718600 | tf_op jit(solution)/shard_map/ppermute | solution.py:274
  69.1 0.7 copy-start
  69.1 0.9 copy-start.1
  69.1 1.0 copy-start.5
  70.2 8.4 %copy-start.14 = (bf16[256,768]{1,0:T(8,128)(2,1)S(1)}, bf16[256,768]{1,0:T(8,128)(2,1)}, u32[]{:S(2)}) copy-start(bf16[256,768]{1,0:T(8,128)(2,1)} %get-tuple-element.32) | copy-start | bytes 1179652
  72.4 50.2 %collective-permute-start.9 = (bf16[8,256,384]{2,1,0:T(8,128)(2,1)}, bf16[8,256,384]{2,1,0:T(8,128)(2,1)S(1)}, u32[]{:S(2)}, u32[]{:S(2)}) collective-permute-start(bf16[8,256,384]{2,1,0:T(8,128)(2,1)} %gather.3), channel_id=1, source_target_pairs={{0,4},{1,5},{2,6},{3,7},{4,8},{5,9},{6,10},{7,11},{8,12},{9,13},{1... | collective-permute-start | bytes 4718600 | tf_op jit(solution)/shard_map/ppermute | solution.py:274
  74.4 49.9 %collective-permute-start.3 = (bf16[256,768]{1,0:T(8,128)(2,1)}, bf16[256,768]{1,0:T(8,128)(2,1)}, u32[]{:S(2)}, u32[]{:S(2)}) collective-permute-start(bf16[256,768]{1,0:T(8,128)(2,1)} %get-tuple-element.30), channel_id=1, source_target_pairs={{0,1},{1,2},{2,3},{3,0},{4,5},{5,6},{6,7},{7,4},{8,9},{9,10},{10,1... | collective-permute-start | bytes 1179656 | tf_op jit(solution)/shard_map/ppermute | solution.py:258
  76.7 47.6 %collective-permute-start.4 = (bf16[256,768]{1,0:T(8,128)(2,1)}, bf16[256,768]{1,0:T(8,128)(2,1)}, u32[]{:S(2)}, u32[]{:S(2)}) collective-permute-start(bf16[256,768]{1,0:T(8,128)(2,1)} %get-tuple-element.31), channel_id=1, source_target_pairs={{0,2},{1,3},{2,0},{3,1},{4,6},{5,7},{6,4},{7,5},{8,10},{9,11},{10,... | collective-permute-start | bytes 1179656 | tf_op jit(solution)/shard_map/ppermute | solution.py:258
  78.6 45.8 %collective-permute-start.5 = (bf16[256,768]{1,0:T(8,128)(2,1)S(1)}, bf16[256,768]{1,0:T(8,128)(2,1)}, u32[]{:S(2)}, u32[]{:S(2)}) collective-permute-start(bf16[256,768]{1,0:T(8,128)(2,1)S(1)} %copy-done.14), channel_id=1, source_target_pairs={{0,3},{1,0},{2,1},{3,2},{4,7},{5,4},{6,5},{7,6},{8,11},{9,8},{10,9... | collective-permute-start | bytes 1179656 | tf_op jit(solution)/shard_map/ppermute | solution.py:258
  82.1 50.3 %collective-permute-start.14 = (bf16[8,256,384]{2,1,0:T(8,128)(2,1)}, bf16[8,256,384]{2,1,0:T(8,128)(2,1)S(1)}, u32[]{:S(2)}, u32[]{:S(2)}) collective-permute-start(bf16[8,256,384]{2,1,0:T(8,128)(2,1)} %collective-permute-done.13.refs_8_), channel_id=1, source_target_pairs={{0,128},{1,129},{2,130},{3,131}} | collective-permute-start | bytes 4718600 | tf_op jit(solution)/shard_map/ppermute | solution.py:277
  122.6 1.1 copy-start.12
  132.4 1.2 copy-start.13
  146.2 18.1 %copy-start.16 = (bf16[256,384]{1,0:T(8,128)(2,1)S(1)}, bf16[256,384]{1,0:T(8,128)(2,1)}, u32[]{:S(2)}) copy-start(bf16[256,384]{1,0:T(8,128)(2,1)} %get-tuple-element.43) | copy-start | bytes 589828
  146.3 19.6 %copy-start.15 = (bf16[256,384]{1,0:T(8,128)(2,1)S(1)}, bf16[256,384]{1,0:T(8,128)(2,1)}, u32[]{:S(2)}) copy-start(bf16[256,384]{1,0:T(8,128)(2,1)} %get-tuple-element.44) | copy-start | bytes 589828
  146.3 24.7 %collective-permute-start.15 = (bf16[256,384]{1,0:T(8,128)(2,1)}, bf16[256,384]{1,0:T(8,128)(2,1)S(1)}, u32[]{:S(2)}, u32[]{:S(2)}) collective-permute-start(bf16[256,384]{1,0:T(8,128)(2,1)} %get-tuple-element.42), channel_id=1, source_target_pairs={{0,3},{1,0},{2,1},{3,2},{4,7},{5,4},{6,5},{7,6},{8,11},{9,8},{10,9... | collective-permute-start | bytes 589832 | tf_op jit(solution)/shard_map/ppermute | solution.py:258
  162.0 20.0 %collective-permute-start.10 = (bf16[256,384]{1,0:T(8,128)(2,1)}, bf16[256,384]{1,0:T(8,128)(2,1)S(1)}, u32[]{:S(2)}, u32[]{:S(2)}) collective-permute-start(bf16[256,384]{1,0:T(8,128)(2,1)} %get-tuple-element.38), channel_id=1, source_target_pairs={{0,3},{1,0},{2,1},{3,2},{4,7},{5,4},{6,5},{7,6},{8,11},{9,8},{10,9... | collective-permute-start | bytes 589832 | tf_op jit(solution)/shard_map/ppermute | solution.py:258
  164.3 10.1 %collective-permute-start.16 = (bf16[256,384]{1,0:T(8,128)(2,1)S(1)}, bf16[256,384]{1,0:T(8,128)(2,1)S(1)}, u32[]{:S(2)}, u32[]{:S(2)}) collective-permute-start(bf16[256,384]{1,0:T(8,128)(2,1)S(1)} %copy-done.16), channel_id=1, source_target_pairs={{0,2},{1,3},{2,0},{3,1},{4,6},{5,7},{6,4},{7,5},{8,10},{9,11},{10,... | collective-permute-start | bytes 589832 | tf_op jit(solution)/shard_map/ppermute | solution.py:258
  165.9 13.5 %collective-permute-start.17 = (bf16[256,384]{1,0:T(8,128)(2,1)S(1)}, bf16[256,384]{1,0:T(8,128)(2,1)S(1)}, u32[]{:S(2)}, u32[]{:S(2)}) collective-permute-start(bf16[256,384]{1,0:T(8,128)(2,1)S(1)} %copy-done.15), channel_id=1, source_target_pairs={{0,1},{1,2},{2,3},{3,0},{4,5},{5,6},{6,7},{7,4},{8,9},{9,10},{10,1... | collective-permute-start | bytes 589832 | tf_op jit(solution)/shard_map/ppermute | solution.py:258
  168.7 13.3 %collective-permute-start.11 = (bf16[256,384]{1,0:T(8,128)(2,1)}, bf16[256,384]{1,0:T(8,128)(2,1)S(1)}, u32[]{:S(2)}, u32[]{:S(2)}) collective-permute-start(bf16[256,384]{1,0:T(8,128)(2,1)} %get-tuple-element.39), channel_id=1, source_target_pairs={{0,2},{1,3},{2,0},{3,1},{4,6},{5,7},{6,4},{7,5},{8,10},{9,11},{10,... | collective-permute-start | bytes 589832 | tf_op jit(solution)/shard_map/ppermute | solution.py:258
  170.9 8.5 %copy-start.6 = (bf16[256,384]{1,0:T(8,128)(2,1)}, bf16[256,384]{1,0:T(8,128)(2,1)S(1)}, u32[]{:S(2)}) copy-start(bf16[256,384]{1,0:T(8,128)(2,1)S(1)} %collective-permute-done.15.refs_1_) | copy-start | bytes 589828
  170.9 17.0 %collective-permute-start.12 = (bf16[256,384]{1,0:T(8,128)(2,1)}, bf16[256,384]{1,0:T(8,128)(2,1)S(1)}, u32[]{:S(2)}, u32[]{:S(2)}) collective-permute-start(bf16[256,384]{1,0:T(8,128)(2,1)} %get-tuple-element.40), channel_id=1, source_target_pairs={{0,1},{1,2},{2,3},{3,0},{4,5},{5,6},{6,7},{7,4},{8,9},{9,10},{10,1... | collective-permute-start | bytes 589832 | tf_op jit(solution)/shard_map/ppermute | solution.py:258
  174.4 5.0 %copy-start.7 = (bf16[256,384]{1,0:T(8,128)(2,1)}, bf16[256,384]{1,0:T(8,128)(2,1)S(1)}, u32[]{:S(2)}) copy-start(bf16[256,384]{1,0:T(8,128)(2,1)S(1)} %collective-permute-done.16.refs_2_) | copy-start | bytes 589828
  179.4 0.7 copy-start.8
  182.0 5.9 %copy-start.9 = (bf16[256,384]{1,0:T(8,128)(2,1)}, bf16[256,384]{1,0:T(8,128)(2,1)S(1)}, u32[]{:S(2)}) copy-start(bf16[256,384]{1,0:T(8,128)(2,1)S(1)} %collective-permute-done.10.refs_1_) | copy-start | bytes 589828
  182.1 5.9 %copy-start.10 = (bf16[256,384]{1,0:T(8,128)(2,1)}, bf16[256,384]{1,0:T(8,128)(2,1)S(1)}, u32[]{:S(2)}) copy-start(bf16[256,384]{1,0:T(8,128)(2,1)S(1)} %collective-permute-done.11.refs_2_) | copy-start | bytes 589828
  187.9 0.7 copy-start.11

commit v3 on v2

--- a/solution.py
+++ b/solution.py
@@ -247,6 +247,7 @@
         scratch_shapes=staging(ways, pieces[0].shape),
         input_output_aliases={ways: 0} if extra else {},
         compiler_params=pltpu.CompilerParams(vmem_limit_bytes=VMEM_LIMIT),
+        cost_estimate=pl.CostEstimate(flops=BUSY, bytes_accessed=0, transcendentals=0),
         name="place",
     )(*pieces, *extra)
 

time: 191 us -> 187 us (0.979)
    ppermute x15, waiting for transfers between devices: 55.7 us -> 52.1 us  [turn(): lax.ppermute(block, 'head', [(i, (i + distance) % ways) for i in range(wa...]
    ppermute x1, waiting for transfers between devices: 8.06 us -> 10.3 us  [onward(): return [block, lax.ppermute(block, ('group', 'head'), last)]]
    unnamed x34 -> x30, local copies, waits for them, and re-layouts: 5.6 us -> 4.48 us
where the time goes in v3:
time: 187 us
  waiting for transfers between devices  102 us (55%)
  starting transfers between devices  41.8 us (22%)
  Pallas kernels  38.6 us (21%)
  local copies, waits for them, and re-layouts  4.48 us (2%)
    ppermute x15, waiting for transfers between devices, turn(): lax.ppermute(block, 'head', [(i, (i + distance) % ways) for i in range(wa...  52.1 us
    ppermute x2, waiting for transfers between devices, onward(): block = lax.ppermute(block, ('group', 'head'), pairs)  39.2 us
    ppermute x15, starting transfers between devices, turn(): lax.ppermute(block, 'head', [(i, (i + distance) % ways) for i in range(wa...  37.2 us
    pallas_call x2, Pallas kernels, attend(): pl.pallas_call(functools.partial(attend_body, ways, chunk, len(priors)),...  24.9 us
    ppermute x1, waiting for transfers between devices, onward(): return [block, lax.ppermute(block, ('group', 'head'), last)]  10.3 us
    pallas_call x1, Pallas kernels, pack(): pl.pallas_call(functools.partial(pack_body, ways, width, order), out_shap...  4.8 us
    unnamed x30, local copies, waits for them, and re-layouts  4.48 us
    pallas_call x2, Pallas kernels, gather(): pl.pallas_call(functools.partial(gather_body, ways), out_shape=jax.ShapeD...  4.46 us
  transfers between devices with their start and end apart: 18, of which 7 were waited for; matrix products, arithmetic and copies ran while one was open for 0% of the time, Pallas kernels for 10%

profile of v3, /device:TPU:32, one launch (start us, length us, event | category | flops | bytes accessed | tf_op | source)
XLA Modules:
  0.0 186.7 jit_solution(7060635641312962667)
XLA Ops:
  0.0 4.8 %pack.1 = (bf16[2,256,384]{2,1,0:T(8,128)(2,1)}, bf16[2,256,384]{2,1,0:T(8,128)(2,1)}, bf16[2,256,384]{2,1,0:T(8,128)(2,1)}, bf16[2,256,384]{2,1,0:T(8,128)(2,1)...) custom-call(bf16[256,3072]{1,0:T(8,128)(2,1)} %refs_0_.1, ...), custom_call_target="tpu_custom_call" | custom-call | tf_op jit(solution)/shard_map/pack/pallas_call | solution.py:99
  4.8 3.3 %collective-permute-start.6 = (bf16[2,256,384]{2,1,0:T(8,128)(2,1)}, bf16[2,256,384]{2,1,0:T(8,128)(2,1)S(1)}, u32[]{:S(2)}, u32[]{:S(2)}) collective-permute-start(bf16[2,256,384]{2,1,0:T(8,128)(2,1)} %get-tuple-element.34), channel_id=1, source_target_pairs={{0,1},{1,2},{2,3},{3,0},{4,5},{5,6},{6,7},{7,4},{8,9},{9,10},{10,1... | collective-permute-start | bytes 1179656 | tf_op jit(solution)/shard_map/ppermute | solution.py:259
  8.2 4.5 %collective-permute-start.7 = (bf16[2,256,384]{2,1,0:T(8,128)(2,1)}, bf16[2,256,384]{2,1,0:T(8,128)(2,1)S(1)}, u32[]{:S(2)}, u32[]{:S(2)}) collective-permute-start(bf16[2,256,384]{2,1,0:T(8,128)(2,1)} %get-tuple-element.35), channel_id=1, source_target_pairs={{0,2},{1,3},{2,0},{3,1},{4,6},{5,7},{6,4},{7,5},{8,10},{9,11},{10,... | collective-permute-start | bytes 1179656 | tf_op jit(solution)/shard_map/ppermute | solution.py:259
  12.7 2.7 %collective-permute-start.8 = (bf16[2,256,384]{2,1,0:T(8,128)(2,1)}, bf16[2,256,384]{2,1,0:T(8,128)(2,1)S(1)}, u32[]{:S(2)}, u32[]{:S(2)}) collective-permute-start(bf16[2,256,384]{2,1,0:T(8,128)(2,1)} %get-tuple-element.36), channel_id=1, source_target_pairs={{0,3},{1,0},{2,1},{3,2},{4,7},{5,4},{6,5},{7,6},{8,11},{9,8},{10,9... | collective-permute-start | bytes 1179656 | tf_op jit(solution)/shard_map/ppermute | solution.py:259
  15.3 0.3 collective-permute-start
  15.6 2.1 %collective-permute-start.1 = (bf16[2,256,384]{2,1,0:T(8,128)(2,1)}, bf16[2,256,384]{2,1,0:T(8,128)(2,1)S(1)}, u32[]{:S(2)}, u32[]{:S(2)}) collective-permute-start(bf16[2,256,384]{2,1,0:T(8,128)(2,1)} %get-tuple-element.27), channel_id=1, source_target_pairs={{0,2},{1,3},{2,0},{3,1},{4,6},{5,7},{6,4},{7,5},{8,10},{9,11},{10,... | collective-permute-start | bytes 1179656 | tf_op jit(solution)/shard_map/ppermute | solution.py:259
  17.7 23.2 %collective-permute-done.6.refs_1_ = bf16[2,256,384]{2,1,0:T(8,128)(2,1)S(1)} collective-permute-done((bf16[2,256,384]{2,1,0:T(8,128)(2,1)}, bf16[2,256,384]{2,1,0:T(8,128)(2,1)S(1)}, u32[]{:S(2)}, u32[]{:S(2)}) %collective-permute-start.6) | collective-permute-done | bytes 393248 | tf_op jit(solution)/shard_map/ppermute | solution.py:259
  40.9 3.0 %collective-permute-start.2 = (bf16[2,256,384]{2,1,0:T(8,128)(2,1)}, bf16[2,256,384]{2,1,0:T(8,128)(2,1)S(1)}, u32[]{:S(2)}, u32[]{:S(2)}) collective-permute-start(bf16[2,256,384]{2,1,0:T(8,128)(2,1)} %get-tuple-element.28), channel_id=1, source_target_pairs={{0,3},{1,0},{2,1},{3,2},{4,7},{5,4},{6,5},{7,6},{8,11},{9,8},{10,9... | collective-permute-start | bytes 1179656 | tf_op jit(solution)/shard_map/ppermute | solution.py:259
  43.8 0.0 collective-permute-done.7.refs_2_
  43.8 0.0 collective-permute-done.8.refs_3_
  43.9 0.8 copy-done.4
  44.6 0.1 copy-done.5
  44.8 2.2 %gather.2.refs_4_ = bf16[8,256,384]{2,1,0:T(8,128)(2,1)} custom-call(bf16[2,256,384]{2,1,0:T(8,128)(2,1)} %get-tuple-element.33.refs_0_, bf16[2,256,384]{2,1,0:T(8,128)(2,1)} %copy-done.3, bf16[2,256,384]{2,1,0:T(8,128)(2,1)} %copy-done.4, bf16[2,256,384]{2,1,0:T(8,128)(2,1)} %copy-done.5), custom_call_target="tpu_custom_call" | custom-call | tf_op jit(solution)/shard_map/gather/pallas_call | solution.py:119
  47.0 1.4 collective-permute-start.13
  48.4 20.8 %collective-permute-done.refs_1_ = bf16[2,256,384]{2,1,0:T(8,128)(2,1)S(1)} collective-permute-done((bf16[2,256,384]{2,1,0:T(8,128)(2,1)}, bf16[2,256,384]{2,1,0:T(8,128)(2,1)S(1)}, u32[]{:S(2)}, u32[]{:S(2)}) %collective-permute-start) | collective-permute-done | bytes 393248 | tf_op jit(solution)/shard_map/ppermute | solution.py:259
  69.2 0.0 collective-permute-done.1.refs_2_
  69.2 0.0 collective-permute-done.2.refs_3_
  69.2 0.7 copy-done
  69.9 0.2 copy-done.1
  70.1 0.2 copy-done.2
  70.2 2.3 %gather.3 = bf16[8,256,384]{2,1,0:T(8,128)(2,1)} custom-call(bf16[2,256,384]{2,1,0:T(8,128)(2,1)} %get-tuple-element.25.refs_0_, bf16[2,256,384]{2,1,0:T(8,128)(2,1)} %copy-done, bf16[2,256,384]{2,1,0:T(8,128)(2,1)} %copy-done.1, bf16[2,256,384]{2,1,0:T(8,128)(2,1)} %copy-done.2, bf16[8,256,384]{2,1,0:T(8,128)(2,1)} %gather.2.refs_4_), custom_call_target="tpu_custom_call" | custom-call | tf_op jit(solution)/shard_map/gather/pallas_call | solution.py:119
  72.5 1.9 %collective-permute-start.9 = (bf16[8,256,384]{2,1,0:T(8,128)(2,1)}, bf16[8,256,384]{2,1,0:T(8,128)(2,1)S(1)}, u32[]{:S(2)}, u32[]{:S(2)}) collective-permute-start(bf16[8,256,384]{2,1,0:T(8,128)(2,1)} %gather.3), channel_id=1, source_target_pairs={{0,4},{1,5},{2,6},{3,7},{4,8},{5,9},{6,10},{7,11},{8,12},{9,13},{1... | collective-permute-start | bytes 4718600 | tf_op jit(solution)/shard_map/ppermute | solution.py:275
  74.4 2.4 %collective-permute-start.3 = (bf16[256,768]{1,0:T(8,128)(2,1)}, bf16[256,768]{1,0:T(8,128)(2,1)}, u32[]{:S(2)}, u32[]{:S(2)}) collective-permute-start(bf16[256,768]{1,0:T(8,128)(2,1)} %get-tuple-element.30), channel_id=1, source_target_pairs={{0,1},{1,2},{2,3},{3,0},{4,5},{5,6},{6,7},{7,4},{8,9},{9,10},{10,1... | collective-permute-start | bytes 1179656 | tf_op jit(solution)/shard_map/ppermute | solution.py:259
  76.8 1.8 collective-permute-start.4
  78.6 3.6 %collective-permute-start.5 = (bf16[256,768]{1,0:T(8,128)(2,1)S(1)}, bf16[256,768]{1,0:T(8,128)(2,1)}, u32[]{:S(2)}, u32[]{:S(2)}) collective-permute-start(bf16[256,768]{1,0:T(8,128)(2,1)S(1)} %copy-done.8), channel_id=1, source_target_pairs={{0,3},{1,0},{2,1},{3,2},{4,7},{5,4},{6,5},{7,6},{8,11},{9,8},{10,9... | collective-permute-start | bytes 1179656 | tf_op jit(solution)/shard_map/ppermute | solution.py:259
  82.2 1.3 collective-permute-start.14
  83.5 39.2 %collective-permute-done.9.refs_0_.refs_8_ = bf16[8,256,384]{2,1,0:T(8,128)(2,1)S(1)} collective-permute-done((bf16[8,256,384]{2,1,0:T(8,128)(2,1)}, bf16[8,256,384]{2,1,0:T(8,128)(2,1)S(1)}, u32[]{:S(2)}, u32[]{:S(2)}) %collective-permute-start.9) | collective-permute-done | bytes 1572896 | tf_op jit(solution)/shard_map/ppermute | solution.py:275
  122.7 1.1 copy-done.6
  123.8 0.5 touch.1.refs_9_.refs_10_
  124.4 0.0 collective-permute-done.4.refs_6_
  124.4 10.3 %collective-permute-done.14.refs_9_ = bf16[8,256,384]{2,1,0:T(8,128)(2,1)} collective-permute-done((bf16[8,256,384]{2,1,0:T(8,128)(2,1)S(1)}, bf16[8,256,384]{2,1,0:T(8,128)(2,1)}, u32[]{:S(2)}, u32[]{:S(2)}) %collective-permute-start.14) | collective-permute-done | bytes 1572896 | tf_op jit(solution)/shard_map/ppermute | solution.py:278
  134.6 12.6 %attend.3 = (bf16[256,384]{1,0:T(8,128)(2,1)}, bf16[256,384]{1,0:T(8,128)(2,1)}, bf16[256,384]{1,0:T(8,128)(2,1)}, bf16[256,384]{1,0:T(8,128)(2,1)}) custom-call(s32[64]{0:T(128)} %noise.3, s32[1,8,16]{2,1,0:T(8,128)} %mask.3, bf16[2,256,384]{2,1,0:T(8,128)(2,1)} %get-tuple-element.33.refs_0_, bf16[2,256,384]{2,1,0:T(8,128)(2,1)} %copy-done.3, ...), custom_call_target="tpu_custom_call" | custom-call | flops 6442450944 | bytes 4718592 | tf_op jit(solution)/shard_map/attend/pallas_call | solution.py:206
  147.3 3.2 %collective-permute-start.15 = (bf16[256,384]{1,0:T(8,128)(2,1)}, bf16[256,384]{1,0:T(8,128)(2,1)S(1)}, u32[]{:S(2)}, u32[]{:S(2)}) collective-permute-start(bf16[256,384]{1,0:T(8,128)(2,1)} %get-tuple-element.42), channel_id=1, source_target_pairs={{0,3},{1,0},{2,1},{3,2},{4,7},{5,4},{6,5},{7,6},{8,11},{9,8},{10,9... | collective-permute-start | bytes 589832 | tf_op jit(solution)/shard_map/ppermute | solution.py:259
  150.5 3.7 %collective-permute-start.16 = (bf16[256,384]{1,0:T(8,128)(2,1)}, bf16[256,384]{1,0:T(8,128)(2,1)S(1)}, u32[]{:S(2)}, u32[]{:S(2)}) collective-permute-start(bf16[256,384]{1,0:T(8,128)(2,1)} %get-tuple-element.43), channel_id=1, source_target_pairs={{0,2},{1,3},{2,0},{3,1},{4,6},{5,7},{6,4},{7,5},{8,10},{9,11},{10,... | collective-permute-start | bytes 589832 | tf_op jit(solution)/shard_map/ppermute | solution.py:259
  154.2 0.9 collective-permute-start.17
  155.1 12.2 %attend.2 = (bf16[256,384]{1,0:T(8,128)(2,1)}, bf16[256,384]{1,0:T(8,128)(2,1)}, bf16[256,384]{1,0:T(8,128)(2,1)}, bf16[256,384]{1,0:T(8,128)(2,1)}) custom-call(s32[64]{0:T(128)} %noise.3, s32[1,8,16]{2,1,0:T(8,128)} %mask.3, bf16[2,256,384]{2,1,0:T(8,128)(2,1)} %get-tuple-element.25.refs_0_, bf16[2,256,384]{2,1,0:T(8,128)(2,1)} %copy-done, ...), custom_call_target="tpu_custom_call" | custom-call | flops 6442450944 | bytes 4718592 | tf_op jit(solution)/shard_map/attend/pallas_call | solution.py:206
  167.3 3.3 %collective-permute-start.10 = (bf16[256,384]{1,0:T(8,128)(2,1)}, bf16[256,384]{1,0:T(8,128)(2,1)S(1)}, u32[]{:S(2)}, u32[]{:S(2)}) collective-permute-start(bf16[256,384]{1,0:T(8,128)(2,1)} %get-tuple-element.38), channel_id=1, source_target_pairs={{0,3},{1,0},{2,1},{3,2},{4,7},{5,4},{6,5},{7,6},{8,11},{9,8},{10,9... | collective-permute-start | bytes 589832 | tf_op jit(solution)/shard_map/ppermute | solution.py:259
  170.7 2.2 %collective-permute-start.11 = (bf16[256,384]{1,0:T(8,128)(2,1)}, bf16[256,384]{1,0:T(8,128)(2,1)S(1)}, u32[]{:S(2)}, u32[]{:S(2)}) collective-permute-start(bf16[256,384]{1,0:T(8,128)(2,1)} %get-tuple-element.39), channel_id=1, source_target_pairs={{0,2},{1,3},{2,0},{3,1},{4,6},{5,7},{6,4},{7,5},{8,10},{9,11},{10,... | collective-permute-start | bytes 589832 | tf_op jit(solution)/shard_map/ppermute | solution.py:259
  172.9 0.3 collective-permute-start.12
  173.1 0.4 copy-done.9
  173.6 0.3 copy-done.10
  173.8 0.1 copy-done.11
  173.9 2.0 %place.2.refs_4_ = bf16[256,3072]{1,0:T(8,128)(2,1)} custom-call(bf16[256,384]{1,0:T(8,128)(2,1)} %get-tuple-element.41.refs_0_, bf16[256,384]{1,0:T(8,128)(2,1)} %copy-done.9, bf16[256,384]{1,0:T(8,128)(2,1)} %copy-done.10, bf16[256,384]{1,0:T(8,128)(2,1)} %copy-done.11), custom_call_target="tpu_custom_call" | custom-call | flops 68719476736 | tf_op jit(solution)/shard_map/place/pallas_call | solution.py:242
  175.8 0.5 collective-permute-done.10.refs_1_
  176.3 6.3 %collective-permute-done.11.refs_2_ = bf16[256,384]{1,0:T(8,128)(2,1)S(1)} collective-permute-done((bf16[256,384]{1,0:T(8,128)(2,1)}, bf16[256,384]{1,0:T(8,128)(2,1)S(1)}, u32[]{:S(2)}, u32[]{:S(2)}) %collective-permute-start.11) | collective-permute-done | bytes 196640 | tf_op jit(solution)/shard_map/ppermute | solution.py:259
  182.6 1.4 collective-permute-done.12.refs_3_
  183.9 0.7 copy-done.14
  184.6 2.0 %place.3 = bf16[256,3072]{1,0:T(8,128)(2,1)} custom-call(bf16[256,384]{1,0:T(8,128)(2,1)} %get-tuple-element.37.refs_0_, bf16[256,384]{1,0:T(8,128)(2,1)} %copy-done.12, bf16[256,384]{1,0:T(8,128)(2,1)} %copy-done.13, bf16[256,384]{1,0:T(8,128)(2,1)} %copy-done.14, bf16[256,3072]{1,0:T(8,128)(2,1)} %place.2.refs_4_), custom_call_target="tpu_custom_call", output_to_operand_aliasing={{}: (4, {})} | custom-call | flops 68719476736 | tf_op jit(solution)/shard_map/place/pallas_call | solution.py:242
  (26 shorter events, 0.1 us)
Async XLA Ops:
  4.8 36.0 %collective-permute-start.6 = (bf16[2,256,384]{2,1,0:T(8,128)(2,1)}, bf16[2,256,384]{2,1,0:T(8,128)(2,1)S(1)}, u32[]{:S(2)}, u32[]{:S(2)}) collective-permute-start(bf16[2,256,384]{2,1,0:T(8,128)(2,1)} %get-tuple-element.34), channel_id=1, source_target_pairs={{0,1},{1,2},{2,3},{3,0},{4,5},{5,6},{6,7},{7,4},{8,9},{9,10},{10,1... | collective-permute-start | bytes 1179656 | tf_op jit(solution)/shard_map/ppermute | solution.py:259
  8.2 35.7 %collective-permute-start.7 = (bf16[2,256,384]{2,1,0:T(8,128)(2,1)}, bf16[2,256,384]{2,1,0:T(8,128)(2,1)S(1)}, u32[]{:S(2)}, u32[]{:S(2)}) collective-permute-start(bf16[2,256,384]{2,1,0:T(8,128)(2,1)} %get-tuple-element.35), channel_id=1, source_target_pairs={{0,2},{1,3},{2,0},{3,1},{4,6},{5,7},{6,4},{7,5},{8,10},{9,11},{10,... | collective-permute-start | bytes 1179656 | tf_op jit(solution)/shard_map/ppermute | solution.py:259
  12.7 31.2 %collective-permute-start.8 = (bf16[2,256,384]{2,1,0:T(8,128)(2,1)}, bf16[2,256,384]{2,1,0:T(8,128)(2,1)S(1)}, u32[]{:S(2)}, u32[]{:S(2)}) collective-permute-start(bf16[2,256,384]{2,1,0:T(8,128)(2,1)} %get-tuple-element.36), channel_id=1, source_target_pairs={{0,3},{1,0},{2,1},{3,2},{4,7},{5,4},{6,5},{7,6},{8,11},{9,8},{10,9... | collective-permute-start | bytes 1179656 | tf_op jit(solution)/shard_map/ppermute | solution.py:259
  15.3 53.9 %collective-permute-start = (bf16[2,256,384]{2,1,0:T(8,128)(2,1)}, bf16[2,256,384]{2,1,0:T(8,128)(2,1)S(1)}, u32[]{:S(2)}, u32[]{:S(2)}) collective-permute-start(bf16[2,256,384]{2,1,0:T(8,128)(2,1)} %get-tuple-element.26), channel_id=1, source_target_pairs={{0,1},{1,2},{2,3},{3,0},{4,5},{5,6},{6,7},{7,4},{8,9},{9,10},{10,1... | collective-permute-start | bytes 1179656 | tf_op jit(solution)/shard_map/ppermute | solution.py:259
  15.6 53.6 %collective-permute-start.1 = (bf16[2,256,384]{2,1,0:T(8,128)(2,1)}, bf16[2,256,384]{2,1,0:T(8,128)(2,1)S(1)}, u32[]{:S(2)}, u32[]{:S(2)}) collective-permute-start(bf16[2,256,384]{2,1,0:T(8,128)(2,1)} %get-tuple-element.27), channel_id=1, source_target_pairs={{0,2},{1,3},{2,0},{3,1},{4,6},{5,7},{6,4},{7,5},{8,10},{9,11},{10,... | collective-permute-start | bytes 1179656 | tf_op jit(solution)/shard_map/ppermute | solution.py:259
  40.9 3.0 %copy-start.3 = (bf16[2,256,384]{2,1,0:T(8,128)(2,1)}, bf16[2,256,384]{2,1,0:T(8,128)(2,1)S(1)}, u32[]{:S(2)}) copy-start(bf16[2,256,384]{2,1,0:T(8,128)(2,1)S(1)} %collective-permute-done.6.refs_1_) | copy-start | bytes 1179652
  40.9 28.3 %collective-permute-start.2 = (bf16[2,256,384]{2,1,0:T(8,128)(2,1)}, bf16[2,256,384]{2,1,0:T(8,128)(2,1)S(1)}, u32[]{:S(2)}, u32[]{:S(2)}) collective-permute-start(bf16[2,256,384]{2,1,0:T(8,128)(2,1)} %get-tuple-element.28), channel_id=1, source_target_pairs={{0,3},{1,0},{2,1},{3,2},{4,7},{5,4},{6,5},{7,6},{8,11},{9,8},{10,9... | collective-permute-start | bytes 1179656 | tf_op jit(solution)/shard_map/ppermute | solution.py:259
  43.8 0.8 copy-start.4
  43.8 0.9 copy-start.5
  47.0 35.2 %collective-permute-start.13 = (bf16[8,256,384]{2,1,0:T(8,128)(2,1)}, bf16[8,256,384]{2,1,0:T(8,128)(2,1)S(1)}, u32[]{:S(2)}, u32[]{:S(2)}) collective-permute-start(bf16[8,256,384]{2,1,0:T(8,128)(2,1)} %gather.2.refs_4_), channel_id=1, source_target_pairs={{0,4},{1,5},{2,6},{3,7},{4,8},{5,9},{6,10},{7,11},{8,12},{9,13},{1... | collective-permute-start | bytes 4718600 | tf_op jit(solution)/shard_map/ppermute | solution.py:275
  69.2 0.7 copy-start
  69.2 0.9 copy-start.1
  69.2 1.0 copy-start.2
  70.2 8.4 %copy-start.8 = (bf16[256,768]{1,0:T(8,128)(2,1)S(1)}, bf16[256,768]{1,0:T(8,128)(2,1)}, u32[]{:S(2)}) copy-start(bf16[256,768]{1,0:T(8,128)(2,1)} %get-tuple-element.32) | copy-start | bytes 1179652
  72.5 50.2 %collective-permute-start.9 = (bf16[8,256,384]{2,1,0:T(8,128)(2,1)}, bf16[8,256,384]{2,1,0:T(8,128)(2,1)S(1)}, u32[]{:S(2)}, u32[]{:S(2)}) collective-permute-start(bf16[8,256,384]{2,1,0:T(8,128)(2,1)} %gather.3), channel_id=1, source_target_pairs={{0,4},{1,5},{2,6},{3,7},{4,8},{5,9},{6,10},{7,11},{8,12},{9,13},{1... | collective-permute-start | bytes 4718600 | tf_op jit(solution)/shard_map/ppermute | solution.py:275
  74.4 49.9 %collective-permute-start.3 = (bf16[256,768]{1,0:T(8,128)(2,1)}, bf16[256,768]{1,0:T(8,128)(2,1)}, u32[]{:S(2)}, u32[]{:S(2)}) collective-permute-start(bf16[256,768]{1,0:T(8,128)(2,1)} %get-tuple-element.30), channel_id=1, source_target_pairs={{0,1},{1,2},{2,3},{3,0},{4,5},{5,6},{6,7},{7,4},{8,9},{9,10},{10,1... | collective-permute-start | bytes 1179656 | tf_op jit(solution)/shard_map/ppermute | solution.py:259
  76.8 47.6 %collective-permute-start.4 = (bf16[256,768]{1,0:T(8,128)(2,1)}, bf16[256,768]{1,0:T(8,128)(2,1)}, u32[]{:S(2)}, u32[]{:S(2)}) collective-permute-start(bf16[256,768]{1,0:T(8,128)(2,1)} %get-tuple-element.31), channel_id=1, source_target_pairs={{0,2},{1,3},{2,0},{3,1},{4,6},{5,7},{6,4},{7,5},{8,10},{9,11},{10,... | collective-permute-start | bytes 1179656 | tf_op jit(solution)/shard_map/ppermute | solution.py:259
  78.6 45.8 %collective-permute-start.5 = (bf16[256,768]{1,0:T(8,128)(2,1)S(1)}, bf16[256,768]{1,0:T(8,128)(2,1)}, u32[]{:S(2)}, u32[]{:S(2)}) collective-permute-start(bf16[256,768]{1,0:T(8,128)(2,1)S(1)} %copy-done.8), channel_id=1, source_target_pairs={{0,3},{1,0},{2,1},{3,2},{4,7},{5,4},{6,5},{7,6},{8,11},{9,8},{10,9... | collective-permute-start | bytes 1179656 | tf_op jit(solution)/shard_map/ppermute | solution.py:259
  82.2 42.2 %copy-start.7 = (bf16[8,256,384]{2,1,0:T(8,128)(2,1)}, bf16[8,256,384]{2,1,0:T(8,128)(2,1)S(1)}, u32[]{:S(2)}) copy-start(bf16[8,256,384]{2,1,0:T(8,128)(2,1)S(1)} %collective-permute-done.13.refs_8_) | copy-start | bytes 4718596
  82.2 52.5 %collective-permute-start.14 = (bf16[8,256,384]{2,1,0:T(8,128)(2,1)S(1)}, bf16[8,256,384]{2,1,0:T(8,128)(2,1)}, u32[]{:S(2)}, u32[]{:S(2)}) collective-permute-start(bf16[8,256,384]{2,1,0:T(8,128)(2,1)S(1)} %collective-permute-done.13.refs_8_), channel_id=1, source_target_pairs={{0,128},{1,129},{2,130},{3,131}} | collective-permute-start | bytes 4718600 | tf_op jit(solution)/shard_map/ppermute | solution.py:278
  122.7 1.1 copy-start.6
  147.3 25.6 %collective-permute-start.15 = (bf16[256,384]{1,0:T(8,128)(2,1)}, bf16[256,384]{1,0:T(8,128)(2,1)S(1)}, u32[]{:S(2)}, u32[]{:S(2)}) collective-permute-start(bf16[256,384]{1,0:T(8,128)(2,1)} %get-tuple-element.42), channel_id=1, source_target_pairs={{0,3},{1,0},{2,1},{3,2},{4,7},{5,4},{6,5},{7,6},{8,11},{9,8},{10,9... | collective-permute-start | bytes 589832 | tf_op jit(solution)/shard_map/ppermute | solution.py:259
  150.5 22.7 %collective-permute-start.16 = (bf16[256,384]{1,0:T(8,128)(2,1)}, bf16[256,384]{1,0:T(8,128)(2,1)S(1)}, u32[]{:S(2)}, u32[]{:S(2)}) collective-permute-start(bf16[256,384]{1,0:T(8,128)(2,1)} %get-tuple-element.43), channel_id=1, source_target_pairs={{0,2},{1,3},{2,0},{3,1},{4,6},{5,7},{6,4},{7,5},{8,10},{9,11},{10,... | collective-permute-start | bytes 589832 | tf_op jit(solution)/shard_map/ppermute | solution.py:259
  154.2 18.9 %collective-permute-start.17 = (bf16[256,384]{1,0:T(8,128)(2,1)}, bf16[256,384]{1,0:T(8,128)(2,1)S(1)}, u32[]{:S(2)}, u32[]{:S(2)}) collective-permute-start(bf16[256,384]{1,0:T(8,128)(2,1)} %get-tuple-element.44), channel_id=1, source_target_pairs={{0,1},{1,2},{2,3},{3,0},{4,5},{5,6},{6,7},{7,4},{8,9},{9,10},{10,1... | collective-permute-start | bytes 589832 | tf_op jit(solution)/shard_map/ppermute | solution.py:259
  167.3 9.0 %collective-permute-start.10 = (bf16[256,384]{1,0:T(8,128)(2,1)}, bf16[256,384]{1,0:T(8,128)(2,1)S(1)}, u32[]{:S(2)}, u32[]{:S(2)}) collective-permute-start(bf16[256,384]{1,0:T(8,128)(2,1)} %get-tuple-element.38), channel_id=1, source_target_pairs={{0,3},{1,0},{2,1},{3,2},{4,7},{5,4},{6,5},{7,6},{8,11},{9,8},{10,9... | collective-permute-start | bytes 589832 | tf_op jit(solution)/shard_map/ppermute | solution.py:259
  170.7 11.9 %collective-permute-start.11 = (bf16[256,384]{1,0:T(8,128)(2,1)}, bf16[256,384]{1,0:T(8,128)(2,1)S(1)}, u32[]{:S(2)}, u32[]{:S(2)}) collective-permute-start(bf16[256,384]{1,0:T(8,128)(2,1)} %get-tuple-element.39), channel_id=1, source_target_pairs={{0,2},{1,3},{2,0},{3,1},{4,6},{5,7},{6,4},{7,5},{8,10},{9,11},{10,... | collective-permute-start | bytes 589832 | tf_op jit(solution)/shard_map/ppermute | solution.py:259
  172.9 0.7 copy-start.9
  172.9 11.1 %collective-permute-start.12 = (bf16[256,384]{1,0:T(8,128)(2,1)}, bf16[256,384]{1,0:T(8,128)(2,1)S(1)}, u32[]{:S(2)}, u32[]{:S(2)}) collective-permute-start(bf16[256,384]{1,0:T(8,128)(2,1)} %get-tuple-element.40), channel_id=1, source_target_pairs={{0,1},{1,2},{2,3},{3,0},{4,5},{5,6},{6,7},{7,4},{8,9},{9,10},{10,1... | collective-permute-start | bytes 589832 | tf_op jit(solution)/shard_map/ppermute | solution.py:259
  173.1 0.7 copy-start.10
  173.1 0.7 copy-start.11
  176.3 7.6 %copy-start.12 = (bf16[256,384]{1,0:T(8,128)(2,1)}, bf16[256,384]{1,0:T(8,128)(2,1)S(1)}, u32[]{:S(2)}) copy-start(bf16[256,384]{1,0:T(8,128)(2,1)S(1)} %collective-permute-done.10.refs_1_) | copy-start | bytes 589828
  182.6 1.4 copy-start.13
  183.9 0.7 copy-start.14
